TPU v7x, 256 devices: a whole 4x4x8 slice. The times are simulated.
256 devices in a mesh: dom: 32 (over x, y, core), spec: 8 (over z).
Axes of the slice: x: 4, y: 4, z: 8, core: 2. Of those that a mesh axis runs over, the one named last changes fastest.
Arguments:
- spectrum: float32 [1296, 32768], P('spec', 'dom'), may hold values from 0.2 to 2
- normals: float32 [2, 3, 65536], P(None, None, 'dom'), may hold values from -3 to 3, as said below
- conn: int32 [3, 65536], P(None, 'dom'), may hold values from 0 to 1535
- send_nodes: int32 [32, 4, 128], P('dom'), may hold values from 0 to 1023, as said below
- step_weight: float32 [32768], P('dom'), may hold values from 0.02 to 0.06
- group_speed: float32 [36], replicated, may hold values from 0.25 to 1
- dia_plus: int32 [1296], replicated, may hold values from 0 to 1295, as said below
- dia_minus: int32 [1296], replicated, may hold values from 0 to 1295, as said below
- dia_coeff: float32 [1296], replicated, may hold values from 0.01 to 0.04
Outputs:
- spectrum_out: float32 [1296, 32768], P(None, ('dom', 'spec'))
Inputs may be any that keep to these rules, and one draw needn't show every extreme that they name: `send_nodes`: each row lists distinct owned nodes of the sending partition. `dia_plus`: for bin f * 36 + d the partner has frequency min(f + 1 or f + 2, 35) and a direction 1 to 3 steps higher, modulo 36. `dia_minus`: for bin f * 36 + d the partner has frequency max(f - 1 or f - 2, 0) and a direction 1 to 3 steps lower, modulo 36. `normals`: for each triangle the three vectors sum to zero and no two are parallel.
All inputs are finite; a program needn't handle non-finite values.
Results may differ from a plain program's by a relative error of at most 0.00002.
Values sent between devices are 32-bit elements; how exact they have to be, the bound alone decides.
A program may use at most 64 MiB of HBM per device.

v0:
```python
import math

import jax
import jax.numpy as jnp
from jax import lax
from jax.sharding import PartitionSpec as P

NDIR = 36
REACH = 2
STEPS = 2


weight_plus = 1.25 ** (-4)
weight_minus = 0.75 ** (-4)
weight_both = 0.9375 ** (-4)


def passed_along(value, axis, steps):
    count = lax.axis_size(axis)
    leading, last = (max(0, -steps), min(count, count - steps))
    return lax.ppermute(value, axis, [(source, source + steps) for source in range(leading, last)])


def corner_terms(normals, speed_east, speed_north):
    coeffs = [
        speed_east[:, None] * normals[0, vertex][None, :]
        + speed_north[:, None] * normals[1, vertex][None, :]
        for vertex in range(3)
    ]
    outward = [jnp.maximum(item, 0.0) for item in coeffs]
    inward = [jnp.minimum(item, 0.0) for item in coeffs]
    denom = inward[0] + inward[1] + inward[2]
    return (outward, inward, denom)


def residual_of(energy, corners, outward, inward, denom):
    values = [jnp.take(energy, corners[vertex], axis=1) for vertex in range(3)]
    inflow = (inward[0] * values[0] + inward[1] * values[1] + inward[2] * values[2]) / denom
    totals = jnp.zeros(energy.shape, jnp.float32)
    for vertex in range(3):
        totals = totals.at[:, corners[vertex]].add(outward[vertex] * (values[vertex] - inflow))
    return totals


def interact(energy, dia_plus, dia_minus, dia_coeff):
    upper = jnp.take(energy, dia_plus, axis=0)
    lower = jnp.take(energy, dia_minus, axis=0)
    term = dia_coeff[:, None] * (
        energy * energy * (weight_plus * upper + weight_minus * lower)
        - 2.0 * weight_both * energy * upper * lower
    )
    change = (-2.0 * term).at[dia_plus].add(term).at[dia_minus].add(term)
    return energy + change


def on_device(
    spectrum, normals, conn, send_nodes, step_weight, group_speed, dia_plus, dia_minus, dia_coeff
):
    row_count = spectrum.shape[0]
    owned_count = spectrum.shape[1]
    slot_size = send_nodes.shape[2]
    send_rows = send_nodes[0]
    offsets = [
        position - REACH if position < REACH else position - REACH + 1
        for position in range(2 * REACH)
    ]
    bins = lax.axis_index("spec") * row_count + jnp.arange(row_count, dtype=jnp.int32)
    freq_of = bins // NDIR
    angle = (bins % NDIR).astype(jnp.float32) * (2.0 * math.pi / NDIR)
    select = (
        freq_of[:, None] == jnp.arange(group_speed.shape[0], dtype=jnp.int32)[None, :]
    ).astype(jnp.float32)
    speed = jnp.sum(select * group_speed[None, :], axis=1)
    outward, inward, denom = corner_terms(normals, speed * jnp.cos(angle), speed * jnp.sin(angle))
    energy = spectrum
    for sweep_index in range(STEPS):
        ghosts = []
        for position in range(2 * REACH):
            piece_out = jnp.take(energy, send_rows[2 * REACH - 1 - position], axis=1)
            ghosts.append(passed_along(piece_out, "dom", -offsets[position]))
        extended = jnp.concatenate([energy] + ghosts, axis=1)
        totals = residual_of(extended, conn, outward, inward, denom)
        own_part = totals[:, :owned_count]
        returned = [
            totals[:, owned_count + position * slot_size : owned_count + (position + 1) * slot_size]
            for position in range(2 * REACH)
        ]
        for position in range(2 * REACH):
            incoming = passed_along(returned[position], "dom", offsets[position])
            own_part = own_part.at[:, send_rows[2 * REACH - 1 - position]].add(incoming)
        energy = energy - step_weight[None, :] * own_part
    node_complete = lax.all_to_all(energy, "spec", split_axis=1, concat_axis=0, tiled=True)
    return interact(node_complete, dia_plus, dia_minus, dia_coeff)


def solution(mesh):
    in_specs = (
        P("spec", "dom"),
        P(None, None, "dom"),
        P(None, "dom"),
        P("dom", None, None),
        P("dom"),
        P(),
        P(),
        P(),
        P(),
    )
    out_specs = P(None, ("dom", "spec"))
    return jax.shard_map(
        on_device, mesh=mesh, in_specs=in_specs, out_specs=out_specs, check_vma=False
    )
```

profile of v0, /device:TPU:1, one launch (start us, length us, event | category | flops | bytes accessed | tf_op | source)
XLA Modules:
  0.0 321.3 jit_solution(8408375436705433884)
XLA Ops:
  0.0 0.8 compare_and_fusion.5
  0.9 1.4 copy.29
  3.2 4.0 %collective-permute-start = (f32[162,128]{0,1:T(8,128)S(1)}, f32[162,128]{0,1:T(8,128)S(1)}, u32[]{:S(2)}, u32[]{:S(2)}) collective-permute-start(f32[162,128]{0,1:T(8,128)S(1)} %select_bitcast_fusion.7), channel_id=1, source_target_pairs={{0,16},{8,24},{16,32},{24,40},{32,48},{40,56},{48,64},{56,72},{64,... | collective-permute-start | bytes 248840 | tf_op jit(solution)/shard_map/ppermute | solution.py:21
  7.3 0.8 gather_fusion.1
  8.1 4.0 %collective-permute-start.1 = (f32[162,128]{0,1:T(8,128)S(1)}, f32[162,128]{0,1:T(8,128)S(1)}, u32[]{:S(2)}, u32[]{:S(2)}) collective-permute-start(f32[162,128]{0,1:T(8,128)S(1)} %select_bitcast_fusion.6), channel_id=1, source_target_pairs={{0,8},{8,16},{16,24},{24,32},{32,40},{40,48},{48,56},{56,64},{64,7... | collective-permute-start | bytes 248840 | tf_op jit(solution)/shard_map/ppermute | solution.py:21
  12.2 0.8 gather_fusion.2
  13.0 1.9 collective-permute-start.2
  16.5 1.3 collective-permute-start.3
  18.3 1.0 collective-permute-done.2
  19.3 4.3 %collective-permute-done.3 = f32[162,128]{0,1:T(8,128)} collective-permute-done((f32[162,128]{0,1:T(8,128)}, f32[162,128]{0,1:T(8,128)}, u32[]{:S(2)}, u32[]{:S(2)}) %collective-permute-start.3) | collective-permute-done | bytes 82976 | tf_op jit(solution)/shard_map/ppermute | solution.py:21
  23.7 0.9 constant_dynamic-update-slice_fusion
  24.6 8.6 %gather_fusion.4 = f32[2048,162]{1,0:T(8,128)} fusion(f32[162,1536]{0,1:T(8,128)S(1)} %constant_dynamic-update-slice_fusion, s32[2048]{0:T(1024)S(1)} %get-tuple-element.54), kind=kCustom, calls=%fused_computation.1.clone | custom fusion | bytes 2662400 | tf_op jit(solution)/shard_map/jit(_take)/gather | solution.py:37
  33.2 8.6 %gather_fusion.5 = f32[2048,162]{1,0:T(8,128)} fusion(f32[162,1536]{0,1:T(8,128)S(1)} %constant_dynamic-update-slice_fusion, s32[2048]{0:T(1024)S(1)} %get-tuple-element.55), kind=kCustom, calls=%fused_computation.10.clone | custom fusion | bytes 2662400 | tf_op jit(solution)/shard_map/jit(_take)/gather | solution.py:37
  41.7 8.6 %gather_fusion.6 = f32[2048,162]{1,0:T(8,128)} fusion(f32[162,1536]{0,1:T(8,128)S(1)} %constant_dynamic-update-slice_fusion, s32[2048]{0:T(1024)S(1)} %fusion.110), kind=kCustom, calls=%fused_computation.11.clone | custom fusion | bytes 2662400 | tf_op jit(solution)/shard_map/jit(_take)/gather | solution.py:37
  50.3 6.6 %fusion.22 = f32[162,2048]{0,1:T(8,128)S(1)} fusion(f32[2048,162]{1,0:T(8,128)} %gather_fusion.6, f32[2048,162]{1,0:T(8,128)} %gather_fusion.5, f32[2048,162]{1,0:T(8,128)} %gather_fusion.4, f32[2048]{0:T(1024)S(1)} %bitcast.176, f32[2048]{0:T(1024)S(1)} %bitcast.180, f32[2048]{0:T(1024)S(1)} %bitcast.184, f32[2048]{0:T(1024)S(1)} %bitcast.188, ...), kind=kLoop, calls=%fused_computation.59 | loop fusion | flops 7630848 | bytes 5365008 | tf_op jit(solution)/shard_map/div | solution.py:38
  56.9 14.8 %scatter_custom_fusion = f32[162,1536]{0,1:T(8,128)} fusion(s32[2048]{0:T(1024)S(1)} %bitcast.210, f32[162,2048]{0,1:T(8,128)S(1)} %fusion.22, f32[2048,162]{1,0:T(8,128)} %gather_fusion.4, f32[]{:T(128)} %constant.16.clone.8, f32[]{:T(128)} %constant.17.clone.1, f32[2048]{0:T(1024)S(1)} %bitcast.197, f32[162]{0:T(256)S(1)} %get-tuple-element.51, ...), kind=kCustom, calls=%fused_computation.54 | custom fusion | flops 2654208 | bytes 5211648 | tf_op jit(solution)/shard_map/scatter-add | solution.py:41
  71.7 16.1 %scatter_custom_fusion.1 = f32[162,1536]{0,1:T(8,128)} fusion(f32[162,1536]{0,1:T(8,128)} %scatter_custom_fusion, s32[2048]{0:T(1024)S(1)} %bitcast.208, f32[162,2048]{0,1:T(8,128)S(1)} %fusion.22, f32[2048,162]{1,0:T(8,128)} %gather_fusion.5, f32[]{:T(128)} %constant.16.clone.8, f32[2048]{0:T(1024)S(1)} %bitcast.185, f32[2048]{0:T(1024)S(1)} %bitcast.189, ...), kind=kCustom, calls=%fused_computation.52 | custom fusion | flops 2654208 | bytes 5211136 | tf_op jit(solution)/shard_map/scatter-add | solution.py:41
  87.8 16.1 %scatter_custom_fusion.2 = f32[162,1536]{0,1:T(8,128)} fusion(f32[162,1536]{0,1:T(8,128)} %scatter_custom_fusion.1, s32[2048]{0:T(1024)S(1)} %bitcast.206, f32[162,2048]{0,1:T(8,128)S(1)} %fusion.22, f32[2048,162]{1,0:T(8,128)} %gather_fusion.6, f32[]{:T(128)} %constant.16.clone.8, f32[2048]{0:T(1024)S(1)} %bitcast.177, f32[2048]{0:T(1024)S(1)} %bitcast.181, ...), kind=kCustom, calls=%fused_computation.50 | custom fusion | flops 2654208 | bytes 5211136 | tf_op jit(solution)/shard_map/scatter-add | solution.py:41
  104.0 1.1 fusion.120
  105.1 1.3 collective-permute-start.4
  106.4 2.8 collective-permute-start.5
  109.2 4.2 %collective-permute-start.6 = (f32[162,128]{0,1:T(8,128)S(1)}, f32[162,128]{0,1:T(8,128)S(1)}, u32[]{:S(2)}, u32[]{:S(2)}) collective-permute-start(f32[162,128]{0,1:T(8,128)S(1)} %get-tuple-element.25), channel_id=1, source_target_pairs={{0,8},{8,16},{16,24},{24,32},{32,40},{40,48},{48,56},{56,64},{64,7... | collective-permute-start | bytes 248840 | tf_op jit(solution)/shard_map/ppermute | solution.py:21
  113.4 3.1 collective-permute-start.7
  116.5 2.3 slice.149
  118.8 3.4 %scatter_custom_fusion.3 = f32[162,1024]{0,1:T(8,128)} fusion(f32[162,1024]{0,1:T(8,128)} %slice.149, s32[128]{0:T(128)S(1)} %get-tuple-element.41, f32[162,128]{0,1:T(8,128)S(1)} %collective-permute-done.4), kind=kCustom, calls=%fused_computation.146 | custom fusion | flops 20736 | bytes 794624 | tf_op jit(solution)/shard_map/scatter-add | solution.py:90
  122.2 3.4 %scatter_custom_fusion.4 = f32[162,1024]{0,1:T(8,128)} fusion(f32[162,1024]{0,1:T(8,128)} %scatter_custom_fusion.3, s32[128]{0:T(128)S(1)} %get-tuple-element.42, f32[162,128]{0,1:T(8,128)S(1)} %collective-permute-done.5), kind=kCustom, calls=%fused_computation.144 | custom fusion | flops 20736 | bytes 794624 | tf_op jit(solution)/shard_map/scatter-add | solution.py:90
  125.6 3.4 %scatter_custom_fusion.5 = f32[162,1024]{0,1:T(8,128)} fusion(f32[162,1024]{0,1:T(8,128)} %scatter_custom_fusion.4, s32[128]{0:T(128)S(1)} %get-tuple-element.43, f32[162,128]{0,1:T(8,128)S(1)} %collective-permute-done.6), kind=kCustom, calls=%fused_computation.142 | custom fusion | flops 20736 | bytes 794624 | tf_op jit(solution)/shard_map/scatter-add | solution.py:90
  128.9 3.4 %scatter_custom_fusion.6 = f32[162,1024]{0,1:T(8,128)} fusion(f32[162,1024]{0,1:T(8,128)} %scatter_custom_fusion.5, s32[128]{0:T(128)S(1)} %get-tuple-element.40, f32[162,128]{0,1:T(8,128)S(1)} %collective-permute-done.7), kind=kCustom, calls=%fused_computation.140 | custom fusion | flops 20736 | bytes 794624 | tf_op jit(solution)/shard_map/scatter-add | solution.py:90
  132.3 2.5 constant_dynamic-update-slice_fusion.9
  134.8 2.1 gather_fusion.7
  136.9 2.0 gather_fusion.8
  138.8 2.0 gather_fusion.9
  141.7 4.5 %collective-permute-start.8 = (f32[162,128]{0,1:T(8,128)S(1)}, f32[162,128]{0,1:T(8,128)S(1)}, u32[]{:S(2)}, u32[]{:S(2)}) collective-permute-start(f32[162,128]{0,1:T(8,128)S(1)} %select_bitcast_fusion.3), channel_id=1, source_target_pairs={{0,16},{8,24},{16,32},{24,40},{32,48},{40,56},{48,64},{56,72},{64,... | collective-permute-start | bytes 248840 | tf_op jit(solution)/shard_map/ppermute | solution.py:21
  146.2 3.0 collective-permute-start.9
  149.3 1.9 collective-permute-start.10
  151.3 1.3 collective-permute-start.11
  152.7 4.4 %collective-permute-done.10 = f32[162,128]{0,1:T(8,128)S(1)} collective-permute-done((f32[162,128]{0,1:T(8,128)S(1)}, f32[162,128]{0,1:T(8,128)S(1)}, u32[]{:S(2)}, u32[]{:S(2)}) %collective-permute-start.10) | collective-permute-done | bytes 82976 | tf_op jit(solution)/shard_map/ppermute | solution.py:21
  157.0 3.4 %collective-permute-done.11 = f32[162,128]{0,1:T(8,128)S(1)} collective-permute-done((f32[162,128]{0,1:T(8,128)S(1)}, f32[162,128]{0,1:T(8,128)S(1)}, u32[]{:S(2)}, u32[]{:S(2)}) %collective-permute-start.11) | collective-permute-done | bytes 82976 | tf_op jit(solution)/shard_map/ppermute | solution.py:21
  160.5 8.6 %gather_fusion.11 = f32[2048,162]{1,0:T(8,128)} fusion(f32[162,1536]{0,1:T(8,128)S(1)} %constant_dynamic-update-slice_fusion.5, s32[2048]{0:T(1024)S(1)} %get-tuple-element.54), kind=kCustom, calls=%fused_computation.12.clone | custom fusion | bytes 2662400 | tf_op jit(solution)/shard_map/jit(_take)/gather | solution.py:37
  169.1 8.6 %gather_fusion.12 = f32[2048,162]{1,0:T(8,128)} fusion(f32[162,1536]{0,1:T(8,128)S(1)} %constant_dynamic-update-slice_fusion.5, s32[2048]{0:T(1024)S(1)} %get-tuple-element.55), kind=kCustom, calls=%fused_computation.13.clone | custom fusion | bytes 2662400 | tf_op jit(solution)/shard_map/jit(_take)/gather | solution.py:37
  177.6 8.6 %gather_fusion.13 = f32[2048,162]{1,0:T(8,128)} fusion(f32[162,1536]{0,1:T(8,128)S(1)} %constant_dynamic-update-slice_fusion.5, s32[2048]{0:T(1024)S(1)} %fusion.110), kind=kCustom, calls=%fused_computation.14.clone | custom fusion | bytes 2662400 | tf_op jit(solution)/shard_map/jit(_take)/gather | solution.py:37
  186.2 6.6 %fusion.7 = f32[162,2048]{0,1:T(8,128)S(1)} fusion(f32[2048,162]{1,0:T(8,128)} %gather_fusion.13, f32[2048,162]{1,0:T(8,128)} %gather_fusion.12, f32[2048,162]{1,0:T(8,128)} %gather_fusion.11, f32[2048]{0:T(1024)S(1)} %bitcast.178, f32[2048]{0:T(1024)S(1)} %bitcast.182, f32[2048]{0:T(1024)S(1)} %bitcast.186, f32[2048]{0:T(1024)S(1)} %bitcast.190, ...), kind=kLoop, calls=%fused_computation.41 | loop fusion | flops 7630848 | bytes 5365008 | tf_op jit(solution)/shard_map/div | solution.py:38
  192.8 14.8 %scatter_custom_fusion.7 = f32[162,1536]{0,1:T(8,128)} fusion(s32[2048]{0:T(1024)S(1)} %bitcast.211, f32[162,2048]{0,1:T(8,128)S(1)} %fusion.7, f32[2048,162]{1,0:T(8,128)} %gather_fusion.11, f32[]{:T(128)} %constant.16.clone.8, f32[]{:T(128)} %constant.17.clone.1, f32[2048]{0:T(1024)S(1)} %bitcast.199, f32[162]{0:T(256)S(1)} %get-tuple-element.51, ...), kind=kCustom, calls=%fused_computation.36 | custom fusion | flops 2654208 | bytes 5211648 | tf_op jit(solution)/shard_map/scatter-add | solution.py:41
  207.6 16.1 %scatter_custom_fusion.8 = f32[162,1536]{0,1:T(8,128)} fusion(f32[162,1536]{0,1:T(8,128)} %scatter_custom_fusion.7, s32[2048]{0:T(1024)S(1)} %bitcast.209, f32[162,2048]{0,1:T(8,128)S(1)} %fusion.7, f32[2048,162]{1,0:T(8,128)} %gather_fusion.12, f32[]{:T(128)} %constant.16.clone.8, f32[2048]{0:T(1024)S(1)} %bitcast.187, f32[2048]{0:T(1024)S(1)} %bitcast.191, ...), kind=kCustom, calls=%fused_computation.34 | custom fusion | flops 2654208 | bytes 5211136 | tf_op jit(solution)/shard_map/scatter-add | solution.py:41
  223.7 16.1 %scatter_custom_fusion.9 = f32[162,1536]{0,1:T(8,128)} fusion(f32[162,1536]{0,1:T(8,128)} %scatter_custom_fusion.8, s32[2048]{0:T(1024)S(1)} %bitcast.207, f32[162,2048]{0,1:T(8,128)S(1)} %fusion.7, f32[2048,162]{1,0:T(8,128)} %gather_fusion.13, f32[]{:T(128)} %constant.16.clone.8, f32[2048]{0:T(1024)S(1)} %bitcast.179, f32[2048]{0:T(1024)S(1)} %bitcast.183, ...), kind=kCustom, calls=%fused_computation.32 | custom fusion | flops 2654208 | bytes 5211136 | tf_op jit(solution)/shard_map/scatter-add | solution.py:41
  239.8 1.1 fusion.119
  241.0 1.3 collective-permute-start.12
  242.3 2.3 collective-permute-start.13
  244.6 4.5 %collective-permute-start.14 = (f32[162,128]{0,1:T(8,128)S(1)}, f32[162,128]{0,1:T(8,128)S(1)}, u32[]{:S(2)}, u32[]{:S(2)}) collective-permute-start(f32[162,128]{0,1:T(8,128)S(1)} %get-tuple-element.21), channel_id=1, source_target_pairs={{0,8},{8,16},{16,24},{24,32},{32,40},{40,48},{48,56},{56,64},{64,7... | collective-permute-start | bytes 248840 | tf_op jit(solution)/shard_map/ppermute | solution.py:21
  249.1 3.6 %collective-permute-start.15 = (f32[162,128]{0,1:T(8,128)S(1)}, f32[162,128]{0,1:T(8,128)S(1)}, u32[]{:S(2)}, u32[]{:S(2)}) collective-permute-start(f32[162,128]{0,1:T(8,128)S(1)} %get-tuple-element.20), channel_id=1, source_target_pairs={{0,16},{8,24},{16,32},{24,40},{32,48},{40,56},{48,64},{56,72},{64,... | collective-permute-start | bytes 248840 | tf_op jit(solution)/shard_map/ppermute | solution.py:21
  252.8 1.3 slice.154
  254.1 1.7 scatter_custom_fusion.10
  255.8 1.7 scatter_custom_fusion.11
  257.5 1.7 scatter_custom_fusion.12
  259.2 1.7 scatter_custom_fusion.13
  261.1 1.2 copy.30
  262.3 8.2 %all-to-all-start = ((f32[162,8,128]{2,0,1:T(8,128)}), f32[162,8,128]{2,0,1:T(8,128)S(1)}, u32[]{:S(2)}, u32[]{:S(2)}) async-start(f32[162,8,128]{2,0,1:T(8,128)} %copy.30), calls=%async_computation | async-start | bytes 1376256 | tf_op jit(solution)/shard_map/all_to_all | solution.py:92
  270.6 21.4 %all-to-all-done = f32[162,8,128]{2,0,1:T(8,128)S(1)} async-done(((f32[162,8,128]{2,0,1:T(8,128)}), f32[162,8,128]{2,0,1:T(8,128)S(1)}, u32[]{:S(2)}, u32[]{:S(2)}) %all-to-all-start) | async-done | bytes 663584 | tf_op jit(solution)/shard_map/all_to_all | solution.py:92
  292.1 2.6 gather_fusion.14
  294.7 3.6 %gather_fusion.15 = f32[1296,128]{1,0:T(8,128)} fusion(f32[1296,128]{1,0:T(8,128)S(1)} %all_to_all.17, s32[2048]{0:T(1024)S(1)} %get-tuple-element.52), kind=kCustom, calls=%fused_computation.15.clone | custom fusion | bytes 1332288 | tf_op jit(solution)/shard_map/jit(_take)/gather | solution.py:47
  298.3 2.7 multiply_add_fusion.3
  301.0 9.4 %scatter_fusion = f32[1296,128]{1,0:T(8,128)S(1)} fusion(f32[1296,128]{1,0:T(8,128)S(1)} %get-tuple-element.6, s32[1296]{0:T(1024)S(1)} %compare_select_fusion.4, f32[1296,128]{1,0:T(8,128)S(1)} %get-tuple-element.8), kind=kCustom, calls=%fused_computation.30 | custom fusion | flops 165888 | bytes 1995840 | tf_op jit(solution)/shard_map/scatter-add | solution.py:52
  310.4 0.8 copy-done
  311.3 10.0 %scatter_fusion.1 = f32[1296,128]{1,0:T(8,128)} fusion(f32[1296,128]{1,0:T(8,128)} %copy-done, s32[1296]{0:T(1024)S(1)} %compare_select_fusion.3, f32[1296,128]{1,0:T(8,128)S(1)} %get-tuple-element.8), kind=kCustom, calls=%fused_computation.31 | custom fusion | flops 165888 | bytes 1995840 | tf_op jit(solution)/shard_map/scatter-add | solution.py:52
  (75 shorter events, 4.4 us)
Async XLA Ops:
  0.8 6.4 %copy-start.9 = (pred[128]{0:T(512)(128)(4,1)}, pred[128]{0:T(512)(128)(4,1)S(1)}, u32[]{:S(2)}) copy-start(pred[128]{0:T(512)(128)(4,1)S(1)} %get-tuple-element.46) | copy-start | bytes 388
  2.3 15.5 %copy-start.2 = (s32[3,2048]{1,0:T(4,128)S(1)}, s32[3,2048]{1,0:T(4,128)}, u32[]{:S(2)}) copy-start(s32[3,2048]{1,0:T(4,128)} %param.17) | copy-start | bytes 73732
  2.3 15.6 %copy-start.11 = (f32[36]{0:T(128)S(1)}, f32[36]{0:T(128)}, u32[]{:S(2)}) copy-start(f32[36]{0:T(128)} %param.20) | copy-start | bytes 436
  2.3 15.8 %copy-start.3 = (f32[2,3,2048]{2,0,1:T(2,128)S(1)}, f32[2,3,2048]{2,0,1:T(2,128)}, u32[]{:S(2)}) copy-start(f32[2,3,2048]{2,0,1:T(2,128)} %param.16) | copy-start | bytes 147460
  3.2 15.0 %collective-permute-start = (f32[162,128]{0,1:T(8,128)S(1)}, f32[162,128]{0,1:T(8,128)S(1)}, u32[]{:S(2)}, u32[]{:S(2)}) collective-permute-start(f32[162,128]{0,1:T(8,128)S(1)} %select_bitcast_fusion.7), channel_id=1, source_target_pairs={{0,16},{8,24},{16,32},{24,40},{32,48},{40,56},{48,64},{56,72},{64,... | collective-permute-start | bytes 248840 | tf_op jit(solution)/shard_map/ppermute | solution.py:21
  8.1 10.1 %collective-permute-start.1 = (f32[162,128]{0,1:T(8,128)S(1)}, f32[162,128]{0,1:T(8,128)S(1)}, u32[]{:S(2)}, u32[]{:S(2)}) collective-permute-start(f32[162,128]{0,1:T(8,128)S(1)} %select_bitcast_fusion.6), channel_id=1, source_target_pairs={{0,8},{8,16},{16,24},{24,32},{32,40},{40,48},{48,56},{56,64},{64,7... | collective-permute-start | bytes 248840 | tf_op jit(solution)/shard_map/ppermute | solution.py:21
  13.0 6.3 %collective-permute-start.2 = (f32[162,128]{0,1:T(8,128)S(1)}, f32[162,128]{0,1:T(8,128)S(1)}, u32[]{:S(2)}, u32[]{:S(2)}) collective-permute-start(f32[162,128]{0,1:T(8,128)S(1)} %select_bitcast_fusion.5), channel_id=1, source_target_pairs={{8,0},{16,8},{24,16},{32,24},{40,32},{48,40},{56,48},{64,56},{72,6... | collective-permute-start | bytes 248840 | tf_op jit(solution)/shard_map/ppermute | solution.py:21
  16.5 7.2 %collective-permute-start.3 = (f32[162,128]{0,1:T(8,128)}, f32[162,128]{0,1:T(8,128)}, u32[]{:S(2)}, u32[]{:S(2)}) collective-permute-start(f32[162,128]{0,1:T(8,128)} %select_bitcast_fusion.4), channel_id=1, source_target_pairs={{16,0},{24,8},{32,16},{40,24},{48,32},{56,40},{64,48},{72,56},{80,... | collective-permute-start | bytes 248840 | tf_op jit(solution)/shard_map/ppermute | solution.py:21
  87.8 28.7 %copy-start.8 = (s32[1,4,128]{2,1,0:T(4,128)S(1)}, s32[1,4,128]{2,1,0:T(4,128)}, u32[]{:S(2)}) copy-start(s32[1,4,128]{2,1,0:T(4,128)} %param.18) | copy-start | bytes 6148
  105.1 13.7 %collective-permute-start.4 = (f32[162,128]{0,1:T(8,128)S(1)}, f32[162,128]{0,1:T(8,128)S(1)}, u32[]{:S(2)}, u32[]{:S(2)}) collective-permute-start(f32[162,128]{0,1:T(8,128)S(1)} %get-tuple-element.27), channel_id=1, source_target_pairs={{16,0},{24,8},{32,16},{40,24},{48,32},{56,40},{64,48},{72,56},{80,... | collective-permute-start | bytes 248840 | tf_op jit(solution)/shard_map/ppermute | solution.py:21
  106.4 15.8 %collective-permute-start.5 = (f32[162,128]{0,1:T(8,128)S(1)}, f32[162,128]{0,1:T(8,128)S(1)}, u32[]{:S(2)}, u32[]{:S(2)}) collective-permute-start(f32[162,128]{0,1:T(8,128)S(1)} %get-tuple-element.26), channel_id=1, source_target_pairs={{8,0},{16,8},{24,16},{32,24},{40,32},{48,40},{56,48},{64,56},{72,6... | collective-permute-start | bytes 248840 | tf_op jit(solution)/shard_map/ppermute | solution.py:21
  109.2 16.4 %collective-permute-start.6 = (f32[162,128]{0,1:T(8,128)S(1)}, f32[162,128]{0,1:T(8,128)S(1)}, u32[]{:S(2)}, u32[]{:S(2)}) collective-permute-start(f32[162,128]{0,1:T(8,128)S(1)} %get-tuple-element.25), channel_id=1, source_target_pairs={{0,8},{8,16},{16,24},{24,32},{32,40},{40,48},{48,56},{56,64},{64,7... | collective-permute-start | bytes 248840 | tf_op jit(solution)/shard_map/ppermute | solution.py:21
  113.4 15.6 %collective-permute-start.7 = (f32[162,128]{0,1:T(8,128)S(1)}, f32[162,128]{0,1:T(8,128)S(1)}, u32[]{:S(2)}, u32[]{:S(2)}) collective-permute-start(f32[162,128]{0,1:T(8,128)S(1)} %get-tuple-element.24), channel_id=1, source_target_pairs={{0,16},{8,24},{16,32},{24,40},{32,48},{40,56},{48,64},{56,72},{64,... | collective-permute-start | bytes 248840 | tf_op jit(solution)/shard_map/ppermute | solution.py:21
  118.8 13.5 %copy-start.6 = (f32[1024]{0:T(1024)S(1)}, f32[1024]{0:T(1024)}, u32[]{:S(2)}) copy-start(f32[1024]{0:T(1024)} %param.19) | copy-start | bytes 12292
  134.8 6.0 %copy-start.1 = (f32[162,1024]{0,1:T(8,128)S(1)}, f32[162,1024]{0,1:T(8,128)}, u32[]{:S(2)}) copy-start(f32[162,1024]{0,1:T(8,128)} %get-tuple-element.11) | copy-start | bytes 1990660
  134.8 6.8 %copy-start.10 = (pred[128]{0:T(512)(128)(4,1)S(1)}, pred[128]{0:T(512)(128)(4,1)}, u32[]{:S(2)}) copy-start(pred[128]{0:T(512)(128)(4,1)} %copy-done.9) | copy-start | bytes 388
  141.7 10.9 %collective-permute-start.8 = (f32[162,128]{0,1:T(8,128)S(1)}, f32[162,128]{0,1:T(8,128)S(1)}, u32[]{:S(2)}, u32[]{:S(2)}) collective-permute-start(f32[162,128]{0,1:T(8,128)S(1)} %select_bitcast_fusion.3), channel_id=1, source_target_pairs={{0,16},{8,24},{16,32},{24,40},{32,48},{40,56},{48,64},{56,72},{64,... | collective-permute-start | bytes 248840 | tf_op jit(solution)/shard_map/ppermute | solution.py:21
  146.2 6.4 %collective-permute-start.9 = (f32[162,128]{0,1:T(8,128)S(1)}, f32[162,128]{0,1:T(8,128)S(1)}, u32[]{:S(2)}, u32[]{:S(2)}) collective-permute-start(f32[162,128]{0,1:T(8,128)S(1)} %select_bitcast_fusion.2), channel_id=1, source_target_pairs={{0,8},{8,16},{16,24},{24,32},{32,40},{40,48},{48,56},{56,64},{64,7... | collective-permute-start | bytes 248840 | tf_op jit(solution)/shard_map/ppermute | solution.py:21
  149.3 7.7 %collective-permute-start.10 = (f32[162,128]{0,1:T(8,128)S(1)}, f32[162,128]{0,1:T(8,128)S(1)}, u32[]{:S(2)}, u32[]{:S(2)}) collective-permute-start(f32[162,128]{0,1:T(8,128)S(1)} %select_bitcast_fusion.1), channel_id=1, source_target_pairs={{8,0},{16,8},{24,16},{32,24},{40,32},{48,40},{56,48},{64,56},{72,6... | collective-permute-start | bytes 248840 | tf_op jit(solution)/shard_map/ppermute | solution.py:21
  151.3 9.2 %collective-permute-start.11 = (f32[162,128]{0,1:T(8,128)S(1)}, f32[162,128]{0,1:T(8,128)S(1)}, u32[]{:S(2)}, u32[]{:S(2)}) collective-permute-start(f32[162,128]{0,1:T(8,128)S(1)} %select_bitcast_fusion), channel_id=1, source_target_pairs={{16,0},{24,8},{32,16},{40,24},{48,32},{56,40},{64,48},{72,56},{80,... | collective-permute-start | bytes 248840 | tf_op jit(solution)/shard_map/ppermute | solution.py:21
  241.0 13.1 %collective-permute-start.12 = (f32[162,128]{0,1:T(8,128)S(1)}, f32[162,128]{0,1:T(8,128)S(1)}, u32[]{:S(2)}, u32[]{:S(2)}) collective-permute-start(f32[162,128]{0,1:T(8,128)S(1)} %get-tuple-element.23), channel_id=1, source_target_pairs={{16,0},{24,8},{32,16},{40,24},{48,32},{56,40},{64,48},{72,56},{80,... | collective-permute-start | bytes 248840 | tf_op jit(solution)/shard_map/ppermute | solution.py:21
  242.3 13.5 %collective-permute-start.13 = (f32[162,128]{0,1:T(8,128)S(1)}, f32[162,128]{0,1:T(8,128)S(1)}, u32[]{:S(2)}, u32[]{:S(2)}) collective-permute-start(f32[162,128]{0,1:T(8,128)S(1)} %get-tuple-element.22), channel_id=1, source_target_pairs={{8,0},{16,8},{24,16},{32,24},{40,32},{48,40},{56,48},{64,56},{72,6... | collective-permute-start | bytes 248840 | tf_op jit(solution)/shard_map/ppermute | solution.py:21
  244.6 12.9 %collective-permute-start.14 = (f32[162,128]{0,1:T(8,128)S(1)}, f32[162,128]{0,1:T(8,128)S(1)}, u32[]{:S(2)}, u32[]{:S(2)}) collective-permute-start(f32[162,128]{0,1:T(8,128)S(1)} %get-tuple-element.21), channel_id=1, source_target_pairs={{0,8},{8,16},{16,24},{24,32},{32,40},{40,48},{48,56},{56,64},{64,7... | collective-permute-start | bytes 248840 | tf_op jit(solution)/shard_map/ppermute | solution.py:21
  249.1 10.1 %collective-permute-start.15 = (f32[162,128]{0,1:T(8,128)S(1)}, f32[162,128]{0,1:T(8,128)S(1)}, u32[]{:S(2)}, u32[]{:S(2)}) collective-permute-start(f32[162,128]{0,1:T(8,128)S(1)} %get-tuple-element.20), channel_id=1, source_target_pairs={{0,16},{8,24},{16,32},{24,40},{32,48},{40,56},{48,64},{56,72},{64,... | collective-permute-start | bytes 248840 | tf_op jit(solution)/shard_map/ppermute | solution.py:21
  261.1 9.4 %copy-start.4 = (s32[1296]{0:T(1024)S(1)}, s32[1296]{0:T(1024)}, u32[]{:S(2)}) copy-start(s32[1296]{0:T(1024)} %param.22) | copy-start | bytes 15556
  261.1 9.4 %copy-start.5 = (s32[1296]{0:T(1024)S(1)}, s32[1296]{0:T(1024)}, u32[]{:S(2)}) copy-start(s32[1296]{0:T(1024)} %param.21) | copy-start | bytes 15556
  262.3 29.7 %all-to-all-start = ((f32[162,8,128]{2,0,1:T(8,128)}), f32[162,8,128]{2,0,1:T(8,128)S(1)}, u32[]{:S(2)}, u32[]{:S(2)}) async-start(f32[162,8,128]{2,0,1:T(8,128)} %copy.30), calls=%async_computation | async-start | bytes 1376256 | tf_op jit(solution)/shard_map/all_to_all | solution.py:92
  294.7 3.7 %copy-start.7 = (f32[1296]{0:T(1024)S(1)}, f32[1296]{0:T(1024)}, u32[]{:S(2)}) copy-start(f32[1296]{0:T(1024)} %param.23) | copy-start | bytes 15556
  310.4 0.8 copy-start
where the time goes:
time: 323 us; the launch traced here: 321 us
  other arithmetic  155 us (48%)
  local copies, waits for them, and re-layouts  77.9 us (24%)
  starting transfers between devices  53.2 us (16%)
  waiting for transfers between devices  34.6 us (11%)
    scatter-add x6, other arithmetic, residual_of(): totals.at[:, corners[vertex]]  94.1 us
    gather x6, local copies, waits for them, and re-layouts, residual_of(): values = [jnp.take(energy, corners[vertex], axis=1) for vertex in range(3)]  51.4 us
    ppermute x16, starting transfers between devices, passed_along(): lax.ppermute(value, axis, [(source, source + steps) for source in range(l...  45.1 us
    all_to_all x1, waiting for transfers between devices, on_device(): lax.all_to_all(energy, 'spec', split_axis=1, concat_axis=0, tiled=True)  21.4 us
    scatter-add x8, other arithmetic, on_device(): own_part = own_part.at[:, send_rows[2 * REACH - 1 - position]].add(incoming)  20.2 us
    scatter-add x2, other arithmetic, interact(): change = (-2.0 * term).at[dia_plus].add(term).at[dia_minus].add(term)  19.4 us
    div x2, other arithmetic, residual_of(): (inward[0] * values[0] + inward[1] * values[1] + inward[2] * values[2]) /...  13.2 us
    ppermute x16, waiting for transfers between devices, passed_along(): lax.ppermute(value, axis, [(source, source + steps) for source in range(l...  13.2 us
  transfers between devices with their start and end apart: 17, of which 5 were waited for; matrix products, arithmetic and copies ran while one was open for 7% of the time, Pallas kernels for 0%

commit v1 on v0

v1 whole, which is shorter than its diff:
```python
import functools
import math

import jax
import jax.numpy as jnp
import numpy as np
from jax import lax
from jax.experimental import pallas as pl
from jax.experimental.pallas import tpu as pltpu
from jax.sharding import PartitionSpec as P

NDIR = 36
NFREQ = 36
BINS = NDIR * NFREQ
STEPS = 2
DOM = 32
SPEC = 8
ROWS = BINS // SPEC
PAD = 168
MAIN = 160
BOTH = 2 * PAD
OWN = 1024
SLOT = 128
BLOCKS = 4
EXT = OWN + BLOCKS * SLOT
ELEM = 2048
CHUNK = 256
CHUNKS = ELEM // CHUNK
TROWS = 88
OFFSETS = (-2, -1, 1, 2)
STRIDE = 48
LEAD = 8
PADDED = (NFREQ + 4) * STRIDE + 8

weight_plus = 1.25 ** (-4)
weight_minus = 0.75 ** (-4)
weight_both = 0.9375 ** (-4)

MESH = pl.DeviceIdType.MESH
f32, bf16 = jnp.float32, jnp.bfloat16


def split(value):
    high = value.astype(bf16).astype(f32)
    low = value - high
    return jnp.concatenate([high[:MAIN], low[:MAIN], high[MAIN:], low[MAIN:]], axis=0).astype(bf16)


def join(value):
    return jnp.concatenate(
        [
            value[:MAIN] + value[MAIN : 2 * MAIN],
            value[2 * MAIN : MAIN + PAD] + value[MAIN + PAD :],
        ],
        axis=0,
    )


def dot(left, right):
    return jnp.dot(left, right, preferred_element_type=f32)


def dot_t(left, right):
    return lax.dot_general(left, right, (((1,), (1,)), ((), ())), preferred_element_type=f32)


def lanes(index, size):
    return pl.ds(pl.multiple_of(index * size, size), size)


def kernel(
    spectrum,
    normals,
    conn,
    send_nodes,
    step_weight,
    group_speed,
    dia_plus,
    dia_minus,
    dia_coeff,
    table,
    out,
    energy,
    parts,
    send_hot,
    corner_hot,
    edge_hot,
    edge_weight,
    edge_diff,
    flux,
    own_sum,
    ghost_out,
    ghost_in,
    back_out,
    back_in,
    landing,
    linear,
    padded,
    term,
    code_plus,
    code_minus,
    coeff,
    halo_send,
    halo_recv,
    spec_send,
    spec_recv,
):
    dom = lax.axis_index("dom")
    spec = lax.axis_index("spec")

    barrier = pltpu.get_barrier_semaphore()
    for offset in OFFSETS:
        pl.semaphore_signal(
            barrier,
            inc=1,
            device_id={"dom": lax.rem(dom + offset + DOM, DOM), "spec": spec},
            device_id_type=MESH,
        )
    for shift in range(1, SPEC):
        pl.semaphore_signal(
            barrier,
            inc=1,
            device_id={"dom": dom, "spec": lax.rem(spec + shift, SPEC)},
            device_id_type=MESH,
        )

    for chunk in range(SPEC):
        energy[chunk, :ROWS] = spectrum[:, chunk * 128 : (chunk + 1) * 128]
        energy[chunk, ROWS:] = jnp.zeros((PAD - ROWS, 128), f32)
        parts[:, chunk * 128 : (chunk + 1) * 128] = split(energy[chunk])

    def hot_rows(rows, index, first=0):
        index = jnp.broadcast_to(index.astype(jnp.int16), (rows, index.shape[1]))
        row = lax.broadcasted_iota(jnp.int16, index.shape, 0) + jnp.int16(first)
        return jnp.where(row == index, bf16(1), bf16(0))

    for row in range(BLOCKS):
        send_hot[:, row * SLOT : (row + 1) * SLOT] = hot_rows(OWN, send_nodes[0, row : row + 1, :])

    pl.semaphore_wait(barrier, BLOCKS + SPEC - 1)

    def ghost_copy(step, row):
        return pltpu.make_async_remote_copy(
            src_ref=ghost_out.at[step, row],
            dst_ref=ghost_in.at[step, BLOCKS - 1 - row],
            send_sem=halo_send.at[step, 0, row],
            recv_sem=halo_recv.at[step, 0, row],
            device_id={"dom": lax.rem(dom + OFFSETS[row] + DOM, DOM), "spec": spec},
            device_id_type=MESH,
        )

    def back_copy(step, block):
        return pltpu.make_async_remote_copy(
            src_ref=back_out.at[step, block],
            dst_ref=back_in.at[step, BLOCKS - 1 - block],
            send_sem=halo_send.at[step, 1, block],
            recv_sem=halo_recv.at[step, 1, block],
            device_id={"dom": lax.rem(dom + OFFSETS[block] + DOM, DOM), "spec": spec},
            device_id_type=MESH,
        )

    def send_ghosts(step):
        pieces = join(dot(parts[:, :OWN], send_hot[...]))
        for row in range(BLOCKS):
            ghost_out[step, row] = pieces[:, row * SLOT : (row + 1) * SLOT]
            ghost_copy(step, row).start()

    def edge_weights(chunk, carry):
        parity = lax.rem(spec, 2) == 0
        east = jnp.where(parity, table[0], table[2])
        north = jnp.where(parity, table[1], table[3])
        at = lanes(chunk, 128)
        k = [
            east * normals[corner, 0:1, at] + north * normals[corner, 1:2, at]
            for corner in range(3)
        ]
        into = [jnp.maximum(value, 0.0) for value in k]
        away = [jnp.maximum(-value, 0.0) for value in k]
        for edge in range(3):
            a, b = edge, (edge + 1) % 3
            edge_weight[edge, :, at] = jnp.minimum(into[a], away[b]) - jnp.minimum(into[b], away[a])
        return carry

    def build_hot(chunk, carry):
        hot = []
        for corner in range(3):
            value = hot_rows(EXT, conn[corner : corner + 1, lanes(chunk, CHUNK)])
            corner_hot[:, lanes(chunk * 3 + corner, CHUNK)] = value
            hot.append(value)
        edge_hot[:, lanes(chunk * 2, CHUNK)] = hot[0] - hot[1]
        edge_hot[:, lanes(chunk * 2 + 1, CHUNK)] = hot[1] - hot[2]
        return carry

    def fluxes(chunk):
        at = lanes(chunk, CHUNK)

        def block(rows, low_rows):
            size = rows.stop - rows.start
            first = rows.start % (2 * NDIR)
            d01 = edge_diff[rows, :CHUNK] + edge_diff[low_rows, :CHUNK]
            d12 = edge_diff[rows, CHUNK:] + edge_diff[low_rows, CHUNK:]
            d20 = -(d01 + d12)
            w01, w12, w20 = [edge_weight[edge, first : first + size, at] for edge in range(3)]
            return [
                jnp.maximum(w01, 0.0) * d01 + jnp.minimum(w20, 0.0) * d20,
                jnp.maximum(w12, 0.0) * d12 + jnp.minimum(w01, 0.0) * d01,
                jnp.maximum(w20, 0.0) * d20 + jnp.minimum(w12, 0.0) * d12,
            ]

        for first in range(0, MAIN, 16):
            rows, low_rows = slice(first, first + 16), slice(MAIN + first, MAIN + first + 16)
            for corner, value in enumerate(block(rows, low_rows)):
                high = value.astype(bf16)
                column = lanes(chunk * 3 + corner, CHUNK)
                flux[rows, column] = high
                flux[low_rows, column] = (value - high.astype(f32)).astype(bf16)
        size = PAD - MAIN
        first = MAIN % (2 * NDIR)
        rows, low_rows = slice(2 * MAIN, 2 * MAIN + size), slice(2 * MAIN + size, BOTH)
        d01 = edge_diff[rows, :CHUNK] + edge_diff[low_rows, :CHUNK]
        d12 = edge_diff[rows, CHUNK:] + edge_diff[low_rows, CHUNK:]
        d20 = -(d01 + d12)
        w01, w12, w20 = [edge_weight[edge, first : first + size, at] for edge in range(3)]
        values = [
            jnp.maximum(w01, 0.0) * d01 + jnp.minimum(w20, 0.0) * d20,
            jnp.maximum(w12, 0.0) * d12 + jnp.minimum(w01, 0.0) * d01,
            jnp.maximum(w20, 0.0) * d20 + jnp.minimum(w12, 0.0) * d12,
        ]
        for corner, value in enumerate(values):
            high = value.astype(bf16).astype(f32)
            column = lanes(chunk * 3 + corner, CHUNK)
            flux[2 * MAIN :, column] = jnp.concatenate([high, value - high], axis=0).astype(bf16)

    def sweep(chunk, carry):
        edge_diff[...] = dot(parts[...], edge_hot[:, lanes(chunk, 2 * CHUNK)])
        fluxes(chunk)
        return carry

    first_bin = spec * ROWS
    first_freq = first_bin // NDIR
    row = lax.broadcasted_iota(jnp.int32, (PAD, 128), 0) + (first_bin - first_freq * NDIR)
    speed = jnp.full((PAD, 128), group_speed[first_freq], f32)
    for later in range(1, 6):
        value = group_speed[jnp.minimum(first_freq + later, NFREQ - 1)]
        speed = jnp.where(row >= later * NDIR, value, speed)

    send_ghosts(0)
    lax.fori_loop(0, CHUNKS, build_hot, 0)
    lax.fori_loop(0, ELEM // 128, edge_weights, 0)

    for step in range(STEPS):
        for block in range(BLOCKS):
            ghost_copy(step, BLOCKS - 1 - block).wait_recv()
            parts[:, OWN + block * SLOT : OWN + (block + 1) * SLOT] = split(ghost_in[step, block])
        lax.fori_loop(0, CHUNKS, sweep, 0)
        ghost_sum = join(dot_t(flux[...], corner_hot[OWN:, :]))
        for block in range(BLOCKS):
            back_out[step, block] = ghost_sum[:, block * SLOT : (block + 1) * SLOT]
            back_copy(step, block).start()

        def own_part(half, carry):
            rows = lanes(half, 512)
            own_sum[:, rows] = join(dot_t(flux[...], corner_hot[rows, :]))
            return carry

        lax.fori_loop(0, 2, own_part, 0)
        for block in range(BLOCKS):
            back_copy(step, block).wait_recv()
        returned = [split(back_in[step, row]) for row in range(BLOCKS)]
        returned = jnp.concatenate(returned, axis=1)
        for half in range(2):
            at = slice(half * 512, (half + 1) * 512)
            total = own_sum[:, at] + join(dot_t(returned, send_hot[at, :]))
            for quarter in range(4):
                chunk = half * 4 + quarter
                weight = step_weight[:, chunk * 128 : (chunk + 1) * 128]
                value = energy[chunk] - (speed * weight) * total[:, quarter * 128 : (quarter + 1) * 128]
                energy[chunk] = value
                if step + 1 < STEPS:
                    parts[:, chunk * 128 : (chunk + 1) * 128] = split(value)
        if step + 1 < STEPS:
            send_ghosts(step + 1)

    def spec_copy(shift):
        to = lax.rem(spec + shift, SPEC)
        return pltpu.make_async_remote_copy(
            src_ref=energy.at[to],
            dst_ref=landing.at[spec],
            send_sem=spec_send.at[shift - 1],
            recv_sem=spec_recv.at[shift - 1],
            device_id={"dom": dom, "spec": to},
            device_id_type=MESH,
        )

    for shift in (4, 3, 5, 2, 6, 1, 7):
        spec_copy(shift).start()
    landing[spec] = energy[spec]

    bin_ = lax.broadcasted_iota(jnp.int32, (1, BINS), 1).astype(f32)
    freq = jnp.floor((bin_ + 0.5) * (1.0 / NDIR))
    direction = bin_ - NDIR * freq

    def partner_code(partner, sign):
        partner = partner.astype(f32)
        other = jnp.floor((partner + 0.5) * (1.0 / NDIR))
        turn = sign * ((partner - NDIR * other) - direction)
        turn = jnp.where(turn < 0, turn + NDIR, turn)
        return 4 * jnp.maximum(sign * (other - freq), 1.0) + turn

    def to_column(value):
        for first in range(0, BINS, 128):
            size = min(128, BINS - first)
            piece = value[:, first : first + size]
            if size < 128:
                piece = jnp.concatenate([piece, jnp.zeros((1, 128 - size), f32)], axis=1)
            linear[first : first + size] = jnp.broadcast_to(piece, (128, 128)).T[:size]

    def to_padded(target):
        def one(f, carry):
            base = pl.multiple_of((f + 2) * STRIDE, 8)
            value = linear[pl.ds(f * NDIR, NDIR)]
            target[pl.ds(base + LEAD, NDIR)] = value
            target[pl.ds(base + LEAD - 3, 3)] = value[NDIR - 3 :]
            target[pl.ds(base + LEAD + NDIR, 3)] = value[:3]
            return carry

        lax.fori_loop(0, NFREQ, one, 0)

    for target, value in (
        (code_plus, partner_code(dia_plus[...], 1.0)),
        (code_minus, partner_code(dia_minus[...], -1.0)),
        (coeff, dia_coeff[...]),
    ):
        target[...] = jnp.zeros((PADDED, 128), f32)
        to_column(value)
        to_padded(target)

    for shift in range(1, SPEC):
        source = lax.rem(spec + SPEC - shift, SPEC)
        pltpu.make_async_remote_copy(
            src_ref=landing.at[source],
            dst_ref=landing.at[source],
            send_sem=spec_send.at[shift - 1],
            recv_sem=spec_recv.at[shift - 1],
            device_id={"dom": dom, "spec": source},
            device_id_type=MESH,
        ).wait_recv()

    half = NDIR // 2
    for source in range(SPEC):
        for piece in range(ROWS // half):
            f, second = divmod(source * (ROWS // half) + piece, 2)
            base = (f + 2) * STRIDE + LEAD
            value = landing[source, piece * half : (piece + 1) * half]
            padded[base + second * half : base + (second + 1) * half] = value
            if second:
                padded[base - 3 : base] = value[half - 3 :]
            else:
                padded[base + NDIR : base + NDIR + 3] = value[:3]
    for block in range(2):
        padded[block * STRIDE : (block + 1) * STRIDE] = padded[2 * STRIDE : 3 * STRIDE]
        last = (NFREQ + 2 + block) * STRIDE
        padded[last : last + STRIDE] = padded[(NFREQ + 1) * STRIDE : (NFREQ + 2) * STRIDE]

    wide = 40
    shifts = [(by, turn) for by in (1, 2) for turn in (1, 2, 3)]

    def terms(f, carry):
        base = pl.multiple_of((f + 2) * STRIDE + LEAD, 8)
        here = padded[pl.ds(base, wide)]
        plus = code_plus[pl.ds(base, wide)]
        minus = code_minus[pl.ds(base, wide)]
        upper = padded[pl.ds(base + STRIDE + 1, wide)]
        lower = padded[pl.ds(base - STRIDE - 1, wide)]
        for by, turn in shifts[1:]:
            code = float(4 * by + turn)
            upper = jnp.where(plus == code, padded[pl.ds(base + by * STRIDE + turn, wide)], upper)
            lower = jnp.where(minus == code, padded[pl.ds(base - by * STRIDE - turn, wide)], lower)
        value = coeff[pl.ds(base, wide)] * (
            here * here * (weight_plus * upper + weight_minus * lower)
            - 2.0 * weight_both * here * upper * lower
        )
        term[pl.ds(base, NDIR)] = value[:NDIR]
        term[pl.ds(base - 3, 3)] = value[NDIR - 3 : NDIR]
        term[pl.ds(base + NDIR, 3)] = value[:3]
        return carry

    lax.fori_loop(0, NFREQ, terms, 0)

    def gained(codes, at, code):
        rows = pl.ds(at, wide)
        return jnp.where(codes[rows] == code, term[rows], 0.0)

    def changes(f, carry):
        base = pl.multiple_of((f + 2) * STRIDE + LEAD, 8)
        value = padded[pl.ds(base, wide)] - 2.0 * term[pl.ds(base, wide)]
        for by, turn in shifts:
            code = float(4 * by + turn)
            value = value + gained(code_plus, base - by * STRIDE - turn, code)
            value = value + gained(code_minus, base + by * STRIDE + turn, code)
        out[pl.ds(f * NDIR, NDIR)] = value[:NDIR]
        return carry

    lax.fori_loop(0, NFREQ, changes, 0)
    high = (NFREQ + 1) * STRIDE + LEAD
    low = 2 * STRIDE + LEAD
    for turn in (1, 2, 3):
        code = float(4 + turn)
        out[BINS - NDIR :] = out[BINS - NDIR :] + gained(code_plus, high - turn, code)[:NDIR]
        out[:NDIR] = out[:NDIR] + gained(code_minus, low + turn, code)[:NDIR]

    for step in range(STEPS):
        for row in range(BLOCKS):
            ghost_copy(step, row).wait_send()
            back_copy(step, row).wait_send()
    for shift in range(1, SPEC):
        spec_copy(shift).wait_send()


def direction_table():
    rows = np.arange(TROWS)
    values = []
    for start in (0, NDIR // 2):
        angle = ((rows + start) % NDIR) * (2.0 * math.pi / NDIR)
        values += [np.cos(angle), np.sin(angle)]
    return np.repeat(np.stack(values)[:, :, None], 128, axis=2).astype(np.float32)


def on_device(
    spectrum, normals, conn, send_nodes, step_weight, group_speed, dia_plus, dia_minus, dia_coeff
):
    vmem = pl.BlockSpec(memory_space=pltpu.VMEM)
    smem = pl.BlockSpec(memory_space=pltpu.SMEM)
    return pl.pallas_call(
        kernel,
        out_shape=jax.ShapeDtypeStruct((BINS, SLOT), f32),
        in_specs=[vmem, vmem, vmem, vmem, vmem, smem, vmem, vmem, vmem, vmem],
        out_specs=vmem,
        scratch_shapes=[
            pltpu.VMEM((SPEC, PAD, 128), f32),
            pltpu.VMEM((BOTH, EXT), bf16),
            pltpu.VMEM((OWN, BLOCKS * SLOT), bf16),
            pltpu.VMEM((EXT, 3 * ELEM), bf16),
            pltpu.VMEM((EXT, 2 * ELEM), bf16),
            pltpu.VMEM((3, TROWS, ELEM), f32),
            pltpu.VMEM((BOTH, 2 * CHUNK), f32),
            pltpu.VMEM((BOTH, 3 * ELEM), bf16),
            pltpu.VMEM((PAD, OWN), f32),
            pltpu.VMEM((STEPS, BLOCKS, PAD, SLOT), f32),
            pltpu.VMEM((STEPS, BLOCKS, PAD, SLOT), f32),
            pltpu.VMEM((STEPS, BLOCKS, PAD, SLOT), f32),
            pltpu.VMEM((STEPS, BLOCKS, PAD, SLOT), f32),
            pltpu.VMEM((SPEC, PAD, 128), f32),
            pltpu.VMEM((BINS + 8, 128), f32),
            pltpu.VMEM((PADDED, 128), f32),
            pltpu.VMEM((PADDED, 128), f32),
            pltpu.VMEM((PADDED, 128), f32),
            pltpu.VMEM((PADDED, 128), f32),
            pltpu.VMEM((PADDED, 128), f32),
            pltpu.SemaphoreType.DMA((STEPS, 2, BLOCKS)),
            pltpu.SemaphoreType.DMA((STEPS, 2, BLOCKS)),
            pltpu.SemaphoreType.DMA((SPEC - 1,)),
            pltpu.SemaphoreType.DMA((SPEC - 1,)),
        ],
        compiler_params=pltpu.CompilerParams(
            collective_id=0, has_side_effects=True, vmem_limit_bytes=62 * 2**20
        ),
    )(
        spectrum,
        jnp.transpose(normals, (1, 0, 2)),
        conn,
        send_nodes,
        step_weight[None, :],
        group_speed,
        dia_plus[None, :],
        dia_minus[None, :],
        dia_coeff[None, :],
        jnp.asarray(direction_table()),
    )


def solution(mesh):
    in_specs = (
        P("spec", "dom"),
        P(None, None, "dom"),
        P(None, "dom"),
        P("dom", None, None),
        P("dom"),
        P(),
        P(),
        P(),
        P(),
    )
    out_specs = P(None, ("dom", "spec"))
    return jax.shard_map(
        on_device, mesh=mesh, in_specs=in_specs, out_specs=out_specs, check_vma=False
    )
```

time: 323 us -> 82.2 us (0.25)
  other arithmetic: 155 us -> 0 us
  Pallas kernels: 0 us -> 77.3 us
  local copies, waits for them, and re-layouts: 77.9 us -> 4.58 us
  starting transfers between devices: 53.2 us -> 0 us
  waiting for transfers between devices: 34.6 us -> 0 us
    scatter-add x16 -> x0, other arithmetic: 134 us -> none  [the longest x6 94.1 us: residual_of(): totals.at[:, corners[vertex]]]
    pallas_call x0 -> x1, Pallas kernels: none -> 77.3 us  [on_device(): pl.pallas_call(kernel, out_shape=jax.ShapeDtypeStruct((BINS, SLOT), f32),...]
    gather x16 -> x0, local copies, waits for them, and re-layouts: 67.4 us -> none  [the longest x6 51.4 us: residual_of(): values = [jnp.take(energy, corners[vertex], axis=1) for vertex in range(3)]]
    ppermute x16 -> x0, starting transfers between devices: 45.1 us -> none  [passed_along(): lax.ppermute(value, axis, [(source, source + steps) for source in range(l...]
    all_to_all x1 -> x0, waiting for transfers between devices: 21.4 us -> none  [on_device(): lax.all_to_all(energy, 'spec', split_axis=1, concat_axis=0, tiled=True)]
    div x2 -> x0, other arithmetic: 13.2 us -> none  [residual_of(): (inward[0] * values[0] + inward[1] * values[1] + inward[2] * values[2]) /...]
    ppermute x16 -> x0, waiting for transfers between devices: 13.2 us -> none  [passed_along(): lax.ppermute(value, axis, [(source, source + steps) for source in range(l...]
    all_to_all x1 -> x0, starting transfers between devices: 8.19 us -> none  [on_device(): lax.all_to_all(energy, 'spec', split_axis=1, concat_axis=0, tiled=True)]
  transfers between devices with their start and end apart: 17 -> 0, of which waited for: 5 -> 0; matrix products, arithmetic and copies ran while one was open for 7% -> 0% of each run, Pallas kernels for 0% -> 0%
where the time goes in v1:
time: 82.2 us; the launch traced here: 81.9 us
  Pallas kernels  77.3 us (94%)
  local copies, waits for them, and re-layouts  4.58 us (6%)
    pallas_call x1, Pallas kernels, on_device(): pl.pallas_call(kernel, out_shape=jax.ShapeDtypeStruct((BINS, SLOT), f32),...  77.3 us
    unnamed x5, local copies, waits for them, and re-layouts  2.08 us

profile of v1, /device:TPU:1, one launch (start us, length us, event | category | flops | bytes accessed | tf_op | source)
XLA Modules:
  0.0 81.9 jit_solution(4547765679090748434)
XLA Ops:
  0.0 0.0 copy-start
  0.0 1.3 %broadcast_in_dim.13.dia_plus = s32[1,1296]{1,0:T(1,128)} reshape(s32[1296]{0:T(1024)} %param.16) | data formatting | bytes 10368 | tf_op jit(solution)/shard_map/broadcast_in_dim | solution.py:475
  1.3 0.0 copy-done
  1.3 0.0 copy-start.1
  1.3 0.6 broadcast_in_dim.14.dia_minus
  1.9 0.1 copy-done.1
  2.0 0.6 broadcast_in_dim.15.dia_coeff
  2.6 77.3 %shard_map.100 = f32[1296,128]{1,0:T(8,128)} custom-call(f32[162,1024]{1,0:T(8,128)} %spectrum.1, f32[3,2,2048]{2,1,0:T(2,128)} %bitcast.2, s32[3,2048]{1,0:T(4,128)} %conn.1, s32[1,4,128]{2,1,0:T(4,128)} %send_nodes.1, f32[1,1024]{1,0:T(1,128)} %bitcast.3, f32[36]{0:T(128)} %group_speed.1, s32[1,1296]{1,0:T(1,128)} %broadcast_in_dim.13.dia_plus, ...), custom_call_target="tpu_custom_call" | custom-call | tf_op jit(solution)/shard_map/pallas_call | solution.py:434
  80.0 2.0 %copy.12 = f32[1296,128]{1,0:T(8,128)} copy(f32[1296,128]{1,0:T(8,128)} %shard_map.100) | data formatting | bytes 1327104
Async XLA Ops:
  0.0 1.3 %copy-start = (s32[1296]{0:T(1024)S(1)}, s32[1296]{0:T(1024)}, u32[]{:S(2)}) copy-start(s32[1296]{0:T(1024)} %param.17) | copy-start | bytes 15556
  1.3 0.7 copy-start.1

commit v2 on v1

--- a/solution.py
+++ b/solution.py
@@ -86,7 +86,9 @@
     corner_hot,
     edge_hot,
     edge_weight,
-    edge_diff,
+    own_diff,
+    even_diff,
+    odd_diff,
     flux,
     own_sum,
     ghost_out,
@@ -137,8 +139,6 @@
     for row in range(BLOCKS):
         send_hot[:, row * SLOT : (row + 1) * SLOT] = hot_rows(OWN, send_nodes[0, row : row + 1, :])
 
-    pl.semaphore_wait(barrier, BLOCKS + SPEC - 1)
-
     def ghost_copy(step, row):
         return pltpu.make_async_remote_copy(
             src_ref=ghost_out.at[step, row],
@@ -159,10 +159,13 @@
             device_id_type=MESH,
         )
 
-    def send_ghosts(step):
+    def make_ghosts(step):
         pieces = join(dot(parts[:, :OWN], send_hot[...]))
         for row in range(BLOCKS):
             ghost_out[step, row] = pieces[:, row * SLOT : (row + 1) * SLOT]
+
+    def send_ghosts(step):
+        for row in range(BLOCKS):
             ghost_copy(step, row).start()
 
     def edge_weights(chunk, carry):
@@ -191,14 +194,28 @@
         edge_hot[:, lanes(chunk * 2 + 1, CHUNK)] = hot[1] - hot[2]
         return carry
 
-    def fluxes(chunk):
+    def own_sweep(chunk, carry):
+        at = lanes(chunk, 1024)
+        own_diff[:, at] = join(dot(parts[:, :OWN], edge_hot[:OWN, at]))
+        return carry
+
+    def ghost_dot(chunk, target):
+        target[...] = dot(parts[:, OWN:], edge_hot[OWN:, lanes(chunk, 2 * CHUNK)])
+
+    def fluxes(chunk, ghost_diff):
         at = lanes(chunk, CHUNK)
 
-        def block(rows, low_rows):
+        def corners(rows, high_rows, low_rows):
             size = rows.stop - rows.start
             first = rows.start % (2 * NDIR)
-            d01 = edge_diff[rows, :CHUNK] + edge_diff[low_rows, :CHUNK]
-            d12 = edge_diff[rows, CHUNK:] + edge_diff[low_rows, CHUNK:]
+            d01, d12 = [
+                own_diff[rows, lanes(2 * chunk + edge, CHUNK)]
+                + (
+                    ghost_diff[high_rows, edge * CHUNK : (edge + 1) * CHUNK]
+                    + ghost_diff[low_rows, edge * CHUNK : (edge + 1) * CHUNK]
+                )
+                for edge in range(2)
+            ]
             d20 = -(d01 + d12)
             w01, w12, w20 = [edge_weight[edge, first : first + size, at] for edge in range(3)]
             return [
@@ -209,31 +226,23 @@
 
         for first in range(0, MAIN, 16):
             rows, low_rows = slice(first, first + 16), slice(MAIN + first, MAIN + first + 16)
-            for corner, value in enumerate(block(rows, low_rows)):
+            for corner, value in enumerate(corners(rows, rows, low_rows)):
                 high = value.astype(bf16)
                 column = lanes(chunk * 3 + corner, CHUNK)
                 flux[rows, column] = high
                 flux[low_rows, column] = (value - high.astype(f32)).astype(bf16)
-        size = PAD - MAIN
-        first = MAIN % (2 * NDIR)
-        rows, low_rows = slice(2 * MAIN, 2 * MAIN + size), slice(2 * MAIN + size, BOTH)
-        d01 = edge_diff[rows, :CHUNK] + edge_diff[low_rows, :CHUNK]
-        d12 = edge_diff[rows, CHUNK:] + edge_diff[low_rows, CHUNK:]
-        d20 = -(d01 + d12)
-        w01, w12, w20 = [edge_weight[edge, first : first + size, at] for edge in range(3)]
-        values = [
-            jnp.maximum(w01, 0.0) * d01 + jnp.minimum(w20, 0.0) * d20,
-            jnp.maximum(w12, 0.0) * d12 + jnp.minimum(w01, 0.0) * d01,
-            jnp.maximum(w20, 0.0) * d20 + jnp.minimum(w12, 0.0) * d12,
-        ]
-        for corner, value in enumerate(values):
+        rows = slice(MAIN, PAD)
+        high_rows, low_rows = slice(2 * MAIN, MAIN + PAD), slice(MAIN + PAD, BOTH)
+        for corner, value in enumerate(corners(rows, high_rows, low_rows)):
             high = value.astype(bf16).astype(f32)
             column = lanes(chunk * 3 + corner, CHUNK)
             flux[2 * MAIN :, column] = jnp.concatenate([high, value - high], axis=0).astype(bf16)
 
-    def sweep(chunk, carry):
-        edge_diff[...] = dot(parts[...], edge_hot[:, lanes(chunk, 2 * CHUNK)])
-        fluxes(chunk)
+    def sweep(pair, carry):
+        ghost_dot(2 * pair + 1, odd_diff)
+        fluxes(2 * pair, even_diff)
+        ghost_dot(2 * pair + 2, even_diff)
+        fluxes(2 * pair + 1, odd_diff)
         return carry
 
     first_bin = spec * ROWS
@@ -244,15 +253,22 @@
         value = group_speed[jnp.minimum(first_freq + later, NFREQ - 1)]
         speed = jnp.where(row >= later * NDIR, value, speed)
 
-    send_ghosts(0)
+    make_ghosts(0)
     lax.fori_loop(0, CHUNKS, build_hot, 0)
     lax.fori_loop(0, ELEM // 128, edge_weights, 0)
+    pl.semaphore_wait(barrier, BLOCKS + SPEC - 1)
+    send_ghosts(0)
 
     for step in range(STEPS):
+        lax.fori_loop(0, ELEM // 512, own_sweep, 0)
         for block in range(BLOCKS):
             ghost_copy(step, BLOCKS - 1 - block).wait_recv()
             parts[:, OWN + block * SLOT : OWN + (block + 1) * SLOT] = split(ghost_in[step, block])
-        lax.fori_loop(0, CHUNKS, sweep, 0)
+        ghost_dot(0, even_diff)
+        lax.fori_loop(0, CHUNKS // 2 - 1, sweep, 0)
+        ghost_dot(CHUNKS - 1, odd_diff)
+        fluxes(CHUNKS - 2, even_diff)
+        fluxes(CHUNKS - 1, odd_diff)
         ghost_sum = join(dot_t(flux[...], corner_hot[OWN:, :]))
         for block in range(BLOCKS):
             back_out[step, block] = ghost_sum[:, block * SLOT : (block + 1) * SLOT]
@@ -279,6 +295,7 @@
                 if step + 1 < STEPS:
                     parts[:, chunk * 128 : (chunk + 1) * 128] = split(value)
         if step + 1 < STEPS:
+            make_ghosts(step + 1)
             send_ghosts(step + 1)
 
     def spec_copy(shift):
@@ -296,24 +313,20 @@
         spec_copy(shift).start()
     landing[spec] = energy[spec]
 
-    bin_ = lax.broadcasted_iota(jnp.int32, (1, BINS), 1).astype(f32)
-    freq = jnp.floor((bin_ + 0.5) * (1.0 / NDIR))
-    direction = bin_ - NDIR * freq
-
-    def partner_code(partner, sign):
+    def partner_code(partner, first, sign):
+        bin_ = lax.broadcasted_iota(jnp.int32, (1, 128), 1).astype(f32) + first
+        freq = jnp.floor((bin_ + 0.5) * (1.0 / NDIR))
         partner = partner.astype(f32)
         other = jnp.floor((partner + 0.5) * (1.0 / NDIR))
-        turn = sign * ((partner - NDIR * other) - direction)
+        turn = sign * ((partner - NDIR * other) - (bin_ - NDIR * freq))
         turn = jnp.where(turn < 0, turn + NDIR, turn)
         return 4 * jnp.maximum(sign * (other - freq), 1.0) + turn
 
-    def to_column(value):
+    def to_column(value, rule):
         for first in range(0, BINS, 128):
-            size = min(128, BINS - first)
-            piece = value[:, first : first + size]
-            if size < 128:
-                piece = jnp.concatenate([piece, jnp.zeros((1, 128 - size), f32)], axis=1)
-            linear[first : first + size] = jnp.broadcast_to(piece, (128, 128)).T[:size]
+            start = min(first, BINS - 128)
+            piece = rule(value[start : start + 128].reshape(1, 128), float(start))
+            linear[start : start + 128] = jnp.broadcast_to(piece, (128, 128)).T
 
     def to_padded(target):
         def one(f, carry):
@@ -326,13 +339,13 @@
 
         lax.fori_loop(0, NFREQ, one, 0)
 
-    for target, value in (
-        (code_plus, partner_code(dia_plus[...], 1.0)),
-        (code_minus, partner_code(dia_minus[...], -1.0)),
-        (coeff, dia_coeff[...]),
+    for target, value, rule in (
+        (code_plus, dia_plus, functools.partial(partner_code, sign=1.0)),
+        (code_minus, dia_minus, functools.partial(partner_code, sign=-1.0)),
+        (coeff, dia_coeff, lambda value, first: value),
     ):
         target[...] = jnp.zeros((PADDED, 128), f32)
-        to_column(value)
+        to_column(value, rule)
         to_padded(target)
 
     for shift in range(1, SPEC):
@@ -443,6 +456,8 @@
             pltpu.VMEM((EXT, 3 * ELEM), bf16),
             pltpu.VMEM((EXT, 2 * ELEM), bf16),
             pltpu.VMEM((3, TROWS, ELEM), f32),
+            pltpu.VMEM((PAD, 2 * ELEM), f32),
+            pltpu.VMEM((BOTH, 2 * CHUNK), f32),
             pltpu.VMEM((BOTH, 2 * CHUNK), f32),
             pltpu.VMEM((BOTH, 3 * ELEM), bf16),
             pltpu.VMEM((PAD, OWN), f32),
@@ -472,9 +487,9 @@
         send_nodes,
         step_weight[None, :],
         group_speed,
-        dia_plus[None, :],
-        dia_minus[None, :],
-        dia_coeff[None, :],
+        dia_plus,
+        dia_minus,
+        dia_coeff,
         jnp.asarray(direction_table()),
     )
 

time: 82.2 us -> 74.6 us (0.908)
  Pallas kernels: 77.3 us -> 72.5 us
  local copies, waits for them, and re-layouts: 4.58 us -> 1.97 us
    pallas_call x1, Pallas kernels: 77.3 us -> 72.5 us  [on_device(): pl.pallas_call(kernel, out_shape=jax.ShapeDtypeStruct((BINS, SLOT), f32),...]
    broadcast_in_dim x3 -> x0, local copies, waits for them, and re-layouts: 2.5 us -> none  [the longest x1 1.31 us: on_device(): dia_plus[None, :]]
    unnamed x5 -> x1, local copies, waits for them, and re-layouts: 2.08 us -> 1.97 us
where the time goes in v2:
time: 74.6 us; the launch traced here: 74.5 us
  Pallas kernels  72.5 us (97%)
  local copies, waits for them, and re-layouts  1.97 us (3%)
    pallas_call x1, Pallas kernels, on_device(): pl.pallas_call(kernel, out_shape=jax.ShapeDtypeStruct((BINS, SLOT), f32),...  72.5 us
    unnamed x1, local copies, waits for them, and re-layouts  1.97 us

profile of v2, /device:TPU:1, one launch (start us, length us, event | category | flops | bytes accessed | tf_op | source)
XLA Modules:
  0.0 74.5 jit_solution(9630917472856060674)
XLA Ops:
  0.0 72.5 %shard_map.100 = f32[1296,128]{1,0:T(8,128)} custom-call(f32[162,1024]{1,0:T(8,128)} %spectrum.1, f32[3,2,2048]{2,1,0:T(2,128)} %bitcast.2, s32[3,2048]{1,0:T(4,128)} %conn.1, s32[1,4,128]{2,1,0:T(4,128)} %send_nodes.1, f32[1,1024]{1,0:T(1,128)} %bitcast.3, f32[36]{0:T(128)} %group_speed.1, s32[1296]{0:T(1024)} %dia_plus.1, s32[1296]{0:T(1024)} %dia_minus.1, ...), custom_call_target="tpu_custom_call" | custom-call | tf_op jit(solution)/shard_map/pallas_call | solution.py:447
  72.5 2.0 %copy.12 = f32[1296,128]{1,0:T(8,128)} copy(f32[1296,128]{1,0:T(8,128)} %shard_map.100) | data formatting | bytes 1327104

commit v3 on v2

v3 whole, which is shorter than its diff:
```python
import functools
import math

import jax
import jax.numpy as jnp
import numpy as np
from jax import lax
from jax.experimental import pallas as pl
from jax.experimental.pallas import tpu as pltpu
from jax.sharding import PartitionSpec as P

NDIR = 36
NFREQ = 36
BINS = NDIR * NFREQ
STEPS = 2
DOM = 32
SPEC = 8
ROWS = BINS // SPEC
GROUPS = 2
MAIN = 80
TAIL = ROWS - 2 * MAIN
PAD = MAIN + 8
PARTS = 256
STEP8 = 16.0
OWN = 1024
SLOT = 128
BLOCKS = 4
EXT = OWN + BLOCKS * SLOT
ELEM = 2048
CHUNK = 256
CHUNKS = ELEM // CHUNK
TROWS = 88
OFFSETS = (-2, -1, 1, 2)
VALUE_LIMIT = 128.0
FLUX_SCALE = 0.25
STRIDE = 48
LEAD = 8
PADDED = (NFREQ + 4) * STRIDE + 8

weight_plus = 1.25 ** (-4)
weight_minus = 0.75 ** (-4)
weight_both = 0.9375 ** (-4)

MESH = pl.DeviceIdType.MESH
f32, bf16, f8 = jnp.float32, jnp.bfloat16, jnp.float8_e4m3fn


def split_two(value):
    high = value.astype(bf16).astype(f32)
    return jnp.concatenate([high, value - high], axis=0).astype(bf16)


def join_two(value):
    return value[:PAD] + value[PAD:]


def three(value):
    second = (value - value.astype(f8).astype(f32)) * STEP8
    third = (second - second.astype(f8).astype(f32)) * STEP8
    return value, second, third


def first_rows(value):
    return jnp.where(lax.broadcasted_iota(jnp.int32, value.shape, 0) < TAIL, value, 0.0)


def tail_parts(value):
    first, second, third = three(first_rows(value))
    return first + pltpu.roll(second, TAIL, 0) + pltpu.roll(third, 2 * TAIL, 0)


def join_tail(value):
    second, third = pltpu.roll(value, 8 - TAIL, 0), pltpu.roll(value, 8 - 2 * TAIL, 0)
    return first_rows(value + (second + third * (1 / STEP8)) * (1 / STEP8))


def split_three(value, group):
    zeros = jnp.zeros((8, value.shape[1]), f32)
    tail = tail_parts(value[MAIN:]) if group else zeros
    return jnp.concatenate([*three(value[:MAIN]), tail, zeros], axis=0).astype(f8)


def join_rows(value, first, size):
    at = [slice(part * MAIN + first, part * MAIN + first + size) for part in range(3)]
    return value[at[0]] + (value[at[1]] + value[at[2]] * (1 / STEP8)) * (1 / STEP8)


def join_three(value, group):
    zeros = jnp.zeros((8, value.shape[1]), f32)
    tail = join_tail(value[3 * MAIN : 3 * MAIN + 8]) if group else zeros
    return jnp.concatenate([join_rows(value, 0, MAIN), tail], axis=0)


def dot(left, right):
    return jnp.dot(left, right, preferred_element_type=f32)


def dot_t(left, right):
    return lax.dot_general(left, right, (((1,), (1,)), ((), ())), preferred_element_type=f32)


def lanes(index, size):
    return pl.ds(pl.multiple_of(index * size, size), size)


def kernel(
    spectrum,
    normals,
    conn,
    send_nodes,
    step_weight,
    group_speed,
    dia_plus,
    dia_minus,
    dia_coeff,
    table,
    out,
    energy,
    whole,
    parts,
    send_hot,
    corner_hot,
    edge_hot,
    edge_weight,
    even_diff,
    odd_diff,
    flux_parts,
    flux,
    own_sum,
    ghost_out,
    ghost_in,
    back_out,
    back_in,
    landing,
    linear,
    padded,
    term,
    code_plus,
    code_minus,
    coeff,
    halo_send,
    halo_recv,
    spec_send,
    spec_recv,
):
    dom = lax.axis_index("dom")
    spec = lax.axis_index("spec")

    barrier = pltpu.get_barrier_semaphore()
    for offset in OFFSETS:
        pl.semaphore_signal(
            barrier,
            inc=1,
            device_id={"dom": lax.rem(dom + offset + DOM, DOM), "spec": spec},
            device_id_type=MESH,
        )
    for shift in range(1, SPEC):
        pl.semaphore_signal(
            barrier,
            inc=1,
            device_id={"dom": dom, "spec": lax.rem(spec + shift, SPEC)},
            device_id_type=MESH,
        )

    for chunk in range(SPEC):
        at = slice(chunk * 128, (chunk + 1) * 128)
        energy[0, chunk, :MAIN] = spectrum[:MAIN, at]
        energy[0, chunk, MAIN:] = jnp.zeros((8, 128), f32)
        energy[1, chunk, : MAIN + TAIL] = spectrum[MAIN:, at]
        energy[1, chunk, MAIN + TAIL :] = jnp.zeros((8 - TAIL, 128), f32)
    flux_parts[3 * MAIN + 8 :] = jnp.zeros((PARTS - 3 * MAIN - 8, 3 * CHUNK), f32)

    for row in range(BLOCKS):
        index = jnp.broadcast_to(send_nodes[0, row : row + 1, :].astype(jnp.int16), (OWN, SLOT))
        node = lax.broadcasted_iota(jnp.int16, index.shape, 0)
        hot = jnp.where(node == index, bf16(1), bf16(0))
        send_hot[:, row * SLOT : (row + 1) * SLOT] = hot

    def halo_copy(group, step, back, block, source, target):
        return pltpu.make_async_remote_copy(
            src_ref=source.at[group, step, block],
            dst_ref=target.at[group, step, BLOCKS - 1 - block],
            send_sem=halo_send.at[group, step, back, block],
            recv_sem=halo_recv.at[group, step, back, block],
            device_id={"dom": lax.rem(dom + OFFSETS[block] + DOM, DOM), "spec": spec},
            device_id_type=MESH,
        )

    def ghost_copy(group, step, row):
        return halo_copy(group, step, 0, row, ghost_out, ghost_in)

    def back_copy(group, step, block):
        return halo_copy(group, step, 1, block, back_out, back_in)

    def make_ghosts(group, step):
        for chunk in range(SPEC):
            whole[:, chunk * 128 : (chunk + 1) * 128] = split_two(energy[group, chunk])
        pieces = join_two(dot(whole[...], send_hot[...]))
        for row in range(BLOCKS):
            ghost_out[group, step, row] = pieces[:, row * SLOT : (row + 1) * SLOT]

    def send_ghosts(group, step):
        for row in range(BLOCKS):
            ghost_copy(group, step, row).start()

    def edge_weights(chunk, carry):
        parity = lax.rem(spec, 2) == 0
        east = jnp.where(parity, table[0], table[2])
        north = jnp.where(parity, table[1], table[3])
        at = lanes(chunk, 128)
        k = [
            east * normals[corner, 0:1, at] + north * normals[corner, 1:2, at]
            for corner in range(3)
        ]
        into = [jnp.maximum(value, 0.0) for value in k]
        away = [jnp.maximum(-value, 0.0) for value in k]
        for edge in range(3):
            a, b = edge, (edge + 1) % 3
            value = jnp.minimum(into[a], away[b]) - jnp.minimum(into[b], away[a])
            edge_weight[edge, :, at] = FLUX_SCALE * value
        return carry

    def build_hot(chunk, carry):
        one, minus, zero = [jnp.full((128, CHUNK), value, f32).astype(f8) for value in (1, -1, 0)]
        node = lax.broadcasted_iota(jnp.int8, (128, CHUNK), 0)
        corners = [conn[corner : corner + 1, lanes(chunk, CHUNK)] for corner in range(3)]
        for first in range(0, EXT, 128):
            rows = slice(first, first + 128)
            hits = []
            for corner in range(3):
                local = corners[corner] - first
                local = jnp.where((local >= 0) & (local < 128), local, -1).astype(jnp.int8)
                hits.append(node == jnp.broadcast_to(local, (128, CHUNK)))
            for corner in range(3):
                value = jnp.where(hits[corner], one, zero)
                corner_hot[rows, lanes(chunk * 3 + corner, CHUNK)] = value
            for edge in range(2):
                a, b = hits[edge], hits[edge + 1]
                value = jnp.where(a, jnp.where(b, zero, one), jnp.where(b, minus, zero))
                edge_hot[rows, lanes(chunk * 2 + edge, CHUNK)] = value
        return carry

    def edge_dot(group, chunk, target):
        target[...] = dot(parts[group], edge_hot[:, lanes(chunk, 2 * CHUNK)])

    def fluxes(group, chunk, diff):
        at = lanes(chunk, CHUNK)

        def corners(first, size, d01, d12):
            start = (group * MAIN + first) % (2 * NDIR)
            d20 = -(d01 + d12)
            w01, w12, w20 = [edge_weight[edge, start : start + size, at] for edge in range(3)]
            return [
                jnp.maximum(w01, 0.0) * d01 + jnp.minimum(w20, 0.0) * d20,
                jnp.maximum(w12, 0.0) * d12 + jnp.minimum(w01, 0.0) * d01,
                jnp.maximum(w20, 0.0) * d20 + jnp.minimum(w12, 0.0) * d12,
            ]

        for first in range(0, MAIN, 16):
            edges = [
                join_rows(diff.at[:, edge * CHUNK : (edge + 1) * CHUNK], first, 16)
                for edge in range(2)
            ]
            for corner, value in enumerate(corners(first, 16, *edges)):
                column = slice(corner * CHUNK, (corner + 1) * CHUNK)
                for part, piece in enumerate(three(value)):
                    flux_parts[part * MAIN + first : part * MAIN + first + 16, column] = piece
        tail = slice(3 * MAIN, 3 * MAIN + 8)
        if group:
            edges = [
                join_tail(diff[tail, edge * CHUNK : (edge + 1) * CHUNK]) for edge in range(2)
            ]
            for corner, value in enumerate(corners(MAIN, 8, *edges)):
                flux_parts[tail, corner * CHUNK : (corner + 1) * CHUNK] = tail_parts(value)
        else:
            flux_parts[tail] = jnp.zeros((8, 3 * CHUNK), f32)
        flux[group, :, lanes(chunk, 3 * CHUNK)] = flux_parts[...].astype(f8)

    def gather(group):
        def pair(index, carry):
            edge_dot(group, 2 * index + 1, odd_diff)
            fluxes(group, 2 * index, even_diff)
            edge_dot(group, 2 * index + 2, even_diff)
            fluxes(group, 2 * index + 1, odd_diff)
            return carry

        edge_dot(group, 0, even_diff)
        lax.fori_loop(0, CHUNKS // 2 - 1, pair, 0)
        edge_dot(group, CHUNKS - 1, odd_diff)
        fluxes(group, CHUNKS - 2, even_diff)
        fluxes(group, CHUNKS - 1, odd_diff)

    first_bin = spec * ROWS
    first_freq = first_bin // NDIR
    speeds = []
    for group in range(GROUPS):
        start = first_bin - first_freq * NDIR + group * MAIN
        row = lax.broadcasted_iota(jnp.int32, (PAD, 128), 0) + start
        speed = jnp.full((PAD, 128), group_speed[first_freq], f32)
        for later in range(1, 6):
            value = group_speed[jnp.minimum(first_freq + later, NFREQ - 1)]
            speed = jnp.where(row >= later * NDIR, value, speed)
        speeds.append(speed)

    unscale = [None] * GROUPS

    def ready(group, step):
        for row in range(BLOCKS):
            ghost_copy(group, step, row).wait_recv()
        chunks = [energy.at[group, chunk] for chunk in range(SPEC)]
        chunks += [ghost_in.at[group, step, block] for block in range(BLOCKS)]
        largest = jnp.abs(chunks[0][...])
        for ref in chunks[1:]:
            largest = jnp.maximum(largest, jnp.abs(ref[...]))
        largest = jnp.maximum(jnp.max(largest, axis=(0, 1), keepdims=True), 1e-30)
        scale = VALUE_LIMIT / largest
        unscale[group] = largest * (1 / (VALUE_LIMIT * FLUX_SCALE))
        for chunk, ref in enumerate(chunks):
            parts[group, :, chunk * 128 : (chunk + 1) * 128] = split_three(ref[...] * scale, group)

    def ghost_scatter(group, step):
        total = dot_t(flux[group], corner_hot[OWN:, :])
        total = join_three(total, group) * unscale[group]
        for block in range(BLOCKS):
            back_out[group, step, block] = total[:, block * SLOT : (block + 1) * SLOT]
            back_copy(group, step, block).start()

    def own_scatter(group):
        def half(index, carry):
            rows = lanes(index, 512)
            own_sum[group, :, rows] = join_three(dot_t(flux[group], corner_hot[rows, :]), group)
            return carry

        lax.fori_loop(0, 2, half, 0)

    def update(group, step):
        for block in range(BLOCKS):
            back_copy(group, step, block).wait_recv()
        returned = [split_two(back_in[group, step, row]) for row in range(BLOCKS)]
        returned = jnp.concatenate(returned, axis=1)
        for half in range(2):
            at = slice(half * 512, (half + 1) * 512)
            total = own_sum[group, :, at] * unscale[group]
            total = total + join_two(dot_t(returned, send_hot[at, :]))
            for quarter in range(4):
                chunk = half * 4 + quarter
                weight = speeds[group] * step_weight[:, chunk * 128 : (chunk + 1) * 128]
                change = weight * total[:, quarter * 128 : (quarter + 1) * 128]
                energy[group, chunk] = energy[group, chunk] - change

    def spec_copy(group, shift):
        to = lax.rem(spec + shift, SPEC)
        count = MAIN + 8 * group
        return pltpu.make_async_remote_copy(
            src_ref=energy.at[group, to, pl.ds(0, count)],
            dst_ref=landing.at[spec, pl.ds(group * MAIN, count)],
            send_sem=spec_send.at[group, shift - 1],
            recv_sem=spec_recv.at[group, shift - 1],
            device_id={"dom": dom, "spec": to},
            device_id_type=MESH,
        )

    def spread(group):
        for shift in (4, 3, 5, 2, 6, 1, 7):
            spec_copy(group, shift).start()
        count = MAIN + 8 * group
        landing[spec, pl.ds(group * MAIN, count)] = energy[group, spec, :count]

    for group in range(GROUPS):
        make_ghosts(group, 0)
    lax.fori_loop(0, CHUNKS, build_hot, 0)
    lax.fori_loop(0, ELEM // 128, edge_weights, 0)
    pl.semaphore_wait(barrier, BLOCKS + SPEC - 1)
    for group in range(GROUPS):
        send_ghosts(group, 0)

    for step in range(STEPS):
        for group in range(GROUPS):
            ready(group, step)
            gather(group)
            ghost_scatter(group, step)
        for group in range(GROUPS):
            own_scatter(group)
            update(group, step)
            if step + 1 < STEPS:
                make_ghosts(group, step + 1)
                send_ghosts(group, step + 1)
            else:
                spread(group)

    def partner_code(partner, first, sign):
        bin_ = lax.broadcasted_iota(jnp.int32, (1, 128), 1).astype(f32) + first
        freq = jnp.floor((bin_ + 0.5) * (1.0 / NDIR))
        partner = partner.astype(f32)
        other = jnp.floor((partner + 0.5) * (1.0 / NDIR))
        turn = sign * ((partner - NDIR * other) - (bin_ - NDIR * freq))
        turn = jnp.where(turn < 0, turn + NDIR, turn)
        return 4 * jnp.maximum(sign * (other - freq), 1.0) + turn

    def to_column(value, rule):
        for first in range(0, BINS, 128):
            start = min(first, BINS - 128)
            piece = rule(value[start : start + 128].reshape(1, 128), float(start))
            linear[start : start + 128] = jnp.broadcast_to(piece, (128, 128)).T

    def to_padded(target):
        def one(f, carry):
            base = pl.multiple_of((f + 2) * STRIDE, 8)
            value = linear[pl.ds(f * NDIR, NDIR)]
            target[pl.ds(base + LEAD, NDIR)] = value
            target[pl.ds(base + LEAD - 3, 3)] = value[NDIR - 3 :]
            target[pl.ds(base + LEAD + NDIR, 3)] = value[:3]
            return carry

        lax.fori_loop(0, NFREQ, one, 0)

    for target, value, rule in (
        (code_plus, dia_plus, functools.partial(partner_code, sign=1.0)),
        (code_minus, dia_minus, functools.partial(partner_code, sign=-1.0)),
        (coeff, dia_coeff, lambda value, first: value),
    ):
        target[...] = jnp.zeros((PADDED, 128), f32)
        to_column(value, rule)
        to_padded(target)

    for group in range(GROUPS):
        for shift in range(1, SPEC):
            source = lax.rem(spec + SPEC - shift, SPEC)
            place = landing.at[source, pl.ds(group * MAIN, MAIN + 8 * group)]
            pltpu.make_async_remote_copy(
                src_ref=place,
                dst_ref=place,
                send_sem=spec_send.at[group, shift - 1],
                recv_sem=spec_recv.at[group, shift - 1],
                device_id={"dom": dom, "spec": source},
                device_id_type=MESH,
            ).wait_recv()

    half = NDIR // 2
    for source in range(SPEC):
        for piece in range(ROWS // half):
            f, second = divmod(source * (ROWS // half) + piece, 2)
            base = (f + 2) * STRIDE + LEAD
            value = landing[source, piece * half : (piece + 1) * half]
            padded[base + second * half : base + (second + 1) * half] = value
            if second:
                padded[base - 3 : base] = value[half - 3 :]
            else:
                padded[base + NDIR : base + NDIR + 3] = value[:3]
    for block in range(2):
        padded[block * STRIDE : (block + 1) * STRIDE] = padded[2 * STRIDE : 3 * STRIDE]
        last = (NFREQ + 2 + block) * STRIDE
        padded[last : last + STRIDE] = padded[(NFREQ + 1) * STRIDE : (NFREQ + 2) * STRIDE]

    wide = 40
    shifts = [(by, turn) for by in (1, 2) for turn in (1, 2, 3)]

    def terms(f, carry):
        base = pl.multiple_of((f + 2) * STRIDE + LEAD, 8)
        here = padded[pl.ds(base, wide)]
        plus = code_plus[pl.ds(base, wide)]
        minus = code_minus[pl.ds(base, wide)]
        upper = padded[pl.ds(base + STRIDE + 1, wide)]
        lower = padded[pl.ds(base - STRIDE - 1, wide)]
        for by, turn in shifts[1:]:
            code = float(4 * by + turn)
            upper = jnp.where(plus == code, padded[pl.ds(base + by * STRIDE + turn, wide)], upper)
            lower = jnp.where(minus == code, padded[pl.ds(base - by * STRIDE - turn, wide)], lower)
        value = coeff[pl.ds(base, wide)] * (
            here * here * (weight_plus * upper + weight_minus * lower)
            - 2.0 * weight_both * here * upper * lower
        )
        term[pl.ds(base, NDIR)] = value[:NDIR]
        term[pl.ds(base - 3, 3)] = value[NDIR - 3 : NDIR]
        term[pl.ds(base + NDIR, 3)] = value[:3]
        return carry

    lax.fori_loop(0, NFREQ, terms, 0)

    def gained(codes, at, code):
        rows = pl.ds(at, wide)
        return jnp.where(codes[rows] == code, term[rows], 0.0)

    def changes(f, carry):
        base = pl.multiple_of((f + 2) * STRIDE + LEAD, 8)
        value = padded[pl.ds(base, wide)] - 2.0 * term[pl.ds(base, wide)]
        for by, turn in shifts:
            code = float(4 * by + turn)
            value = value + gained(code_plus, base - by * STRIDE - turn, code)
            value = value + gained(code_minus, base + by * STRIDE + turn, code)
        out[pl.ds(f * NDIR, NDIR)] = value[:NDIR]
        return carry

    lax.fori_loop(0, NFREQ, changes, 0)
    high = (NFREQ + 1) * STRIDE + LEAD
    low = 2 * STRIDE + LEAD
    for turn in (1, 2, 3):
        code = float(4 + turn)
        out[BINS - NDIR :] = out[BINS - NDIR :] + gained(code_plus, high - turn, code)[:NDIR]
        out[:NDIR] = out[:NDIR] + gained(code_minus, low + turn, code)[:NDIR]

    for group in range(GROUPS):
        for step in range(STEPS):
            for row in range(BLOCKS):
                ghost_copy(group, step, row).wait_send()
                back_copy(group, step, row).wait_send()
        for shift in range(1, SPEC):
            spec_copy(group, shift).wait_send()


def direction_table():
    rows = np.arange(TROWS)
    values = []
    for start in (0, NDIR // 2):
        angle = ((rows + start) % NDIR) * (2.0 * math.pi / NDIR)
        values += [np.cos(angle), np.sin(angle)]
    return np.repeat(np.stack(values)[:, :, None], 128, axis=2).astype(np.float32)


def on_device(
    spectrum, normals, conn, send_nodes, step_weight, group_speed, dia_plus, dia_minus, dia_coeff
):
    vmem = pl.BlockSpec(memory_space=pltpu.VMEM)
    smem = pl.BlockSpec(memory_space=pltpu.SMEM)
    return pl.pallas_call(
        kernel,
        out_shape=jax.ShapeDtypeStruct((BINS, SLOT), f32),
        in_specs=[vmem, vmem, vmem, vmem, vmem, smem, vmem, vmem, vmem, vmem],
        out_specs=vmem,
        scratch_shapes=[
            pltpu.VMEM((GROUPS, SPEC, PAD, 128), f32),
            pltpu.VMEM((2 * PAD, OWN), bf16),
            pltpu.VMEM((GROUPS, PARTS, EXT), f8),
            pltpu.VMEM((OWN, BLOCKS * SLOT), bf16),
            pltpu.VMEM((EXT, 3 * ELEM), f8),
            pltpu.VMEM((EXT, 2 * ELEM), f8),
            pltpu.VMEM((3, TROWS, ELEM), f32),
            pltpu.VMEM((PARTS, 2 * CHUNK), f32),
            pltpu.VMEM((PARTS, 2 * CHUNK), f32),
            pltpu.VMEM((PARTS, 3 * CHUNK), f32),
            pltpu.VMEM((GROUPS, PARTS, 3 * ELEM), f8),
            pltpu.VMEM((GROUPS, PAD, OWN), f32),
            pltpu.VMEM((GROUPS, STEPS, BLOCKS, PAD, SLOT), f32),
            pltpu.VMEM((GROUPS, STEPS, BLOCKS, PAD, SLOT), f32),
            pltpu.VMEM((GROUPS, STEPS, BLOCKS, PAD, SLOT), f32),
            pltpu.VMEM((GROUPS, STEPS, BLOCKS, PAD, SLOT), f32),
            pltpu.VMEM((SPEC, ROWS + 6, 128), f32),
            pltpu.VMEM((BINS + 8, 128), f32),
            pltpu.VMEM((PADDED, 128), f32),
            pltpu.VMEM((PADDED, 128), f32),
            pltpu.VMEM((PADDED, 128), f32),
            pltpu.VMEM((PADDED, 128), f32),
            pltpu.VMEM((PADDED, 128), f32),
            pltpu.SemaphoreType.DMA((GROUPS, STEPS, 2, BLOCKS)),
            pltpu.SemaphoreType.DMA((GROUPS, STEPS, 2, BLOCKS)),
            pltpu.SemaphoreType.DMA((GROUPS, SPEC - 1)),
            pltpu.SemaphoreType.DMA((GROUPS, SPEC - 1)),
        ],
        compiler_params=pltpu.CompilerParams(
            collective_id=0, has_side_effects=True, vmem_limit_bytes=62 * 2**20
        ),
    )(
        spectrum,
        jnp.transpose(normals, (1, 0, 2)),
        conn,
        send_nodes,
        step_weight[None, :],
        group_speed,
        dia_plus,
        dia_minus,
        dia_coeff,
        jnp.asarray(direction_table()),
    )


def solution(mesh):
    in_specs = (
        P("spec", "dom"),
        P(None, None, "dom"),
        P(None, "dom"),
        P("dom", None, None),
        P("dom"),
        P(),
        P(),
        P(),
        P(),
    )
    out_specs = P(None, ("dom", "spec"))
    return jax.shard_map(
        on_device, mesh=mesh, in_specs=in_specs, out_specs=out_specs, check_vma=False
    )
```

time: 74.6 us -> 67.8 us (0.909)
  Pallas kernels: 72.5 us -> 65.7 us
    pallas_call x1, Pallas kernels: 72.5 us -> 65.7 us  [on_device(): pl.pallas_call(kernel, out_shape=jax.ShapeDtypeStruct((BINS, SLOT), f32),...]
where the time goes in v3:
time: 67.8 us; the launch traced here: 67.7 us
  Pallas kernels  65.7 us (97%)
  local copies, waits for them, and re-layouts  1.97 us (3%)
    pallas_call x1, Pallas kernels, on_device(): pl.pallas_call(kernel, out_shape=jax.ShapeDtypeStruct((BINS, SLOT), f32),...  65.7 us
    unnamed x1, local copies, waits for them, and re-layouts  1.97 us

profile of v3, /device:TPU:1, one launch (start us, length us, event | category | flops | bytes accessed | tf_op | source)
XLA Modules:
  0.0 67.7 jit_solution(10857166816474519160)
XLA Ops:
  0.0 65.7 %shard_map.100 = f32[1296,128]{1,0:T(8,128)} custom-call(f32[162,1024]{1,0:T(8,128)} %spectrum.1, f32[3,2,2048]{2,1,0:T(2,128)} %bitcast.2, s32[3,2048]{1,0:T(4,128)} %conn.1, s32[1,4,128]{2,1,0:T(4,128)} %send_nodes.1, f32[1,1024]{1,0:T(1,128)} %bitcast.3, f32[36]{0:T(128)} %group_speed.1, s32[1296]{0:T(1024)} %dia_plus.1, s32[1296]{0:T(1024)} %dia_minus.1, ...), custom_call_target="tpu_custom_call" | custom-call | tf_op jit(solution)/shard_map/pallas_call | solution.py:525
  65.7 2.0 %copy.12 = f32[1296,128]{1,0:T(8,128)} copy(f32[1296,128]{1,0:T(8,128)} %shard_map.100) | data formatting | bytes 1327104

commit v4 on v3

--- a/solution.py
+++ b/solution.py
@@ -32,7 +32,8 @@
 TROWS = 88
 OFFSETS = (-2, -1, 1, 2)
 VALUE_LIMIT = 128.0
-FLUX_SCALE = 0.25
+FLUX_LIMIT = 240.0
+WHOLE = 1.5 * 2.0**23
 STRIDE = 48
 LEAD = 8
 PADDED = (NFREQ + 4) * STRIDE + 8
@@ -54,10 +55,16 @@
     return value[:PAD] + value[PAD:]
 
 
+def whole_number(value):
+    return (value + WHOLE) - WHOLE
+
+
 def three(value):
-    second = (value - value.astype(f8).astype(f32)) * STEP8
-    third = (second - second.astype(f8).astype(f32)) * STEP8
-    return value, second, third
+    first = whole_number(value)
+    rest = (value - first.astype(f8).astype(f32)) * STEP8
+    second = whole_number(rest)
+    third = (rest - second.astype(f8).astype(f32)) * STEP8
+    return first, second, third
 
 
 def first_rows(value):
@@ -203,6 +210,10 @@
         for row in range(BLOCKS):
             ghost_copy(group, step, row).start()
 
+    longest = normals[:, 0] * normals[:, 0] + normals[:, 1] * normals[:, 1]
+    longest = jnp.sqrt(jnp.max(longest, axis=(0, 1), keepdims=True))
+    flux_scale = (FLUX_LIMIT / (2 * VALUE_LIMIT)) / longest
+
     def edge_weights(chunk, carry):
         parity = lax.rem(spec, 2) == 0
         east = jnp.where(parity, table[0], table[2])
@@ -217,7 +228,7 @@
         for edge in range(3):
             a, b = edge, (edge + 1) % 3
             value = jnp.minimum(into[a], away[b]) - jnp.minimum(into[b], away[a])
-            edge_weight[edge, :, at] = FLUX_SCALE * value
+            edge_weight[edge, :, at] = flux_scale * value
         return carry
 
     def build_hot(chunk, carry):
@@ -309,14 +320,23 @@
             ghost_copy(group, step, row).wait_recv()
         chunks = [energy.at[group, chunk] for chunk in range(SPEC)]
         chunks += [ghost_in.at[group, step, block] for block in range(BLOCKS)]
-        largest = jnp.abs(chunks[0][...])
-        for ref in chunks[1:]:
-            largest = jnp.maximum(largest, jnp.abs(ref[...]))
-        largest = jnp.maximum(jnp.max(largest, axis=(0, 1), keepdims=True), 1e-30)
-        scale = VALUE_LIMIT / largest
-        unscale[group] = largest * (1 / (VALUE_LIMIT * FLUX_SCALE))
+        most = least = chunks[0][:MAIN]
+        for ref in chunks:
+            most = jnp.maximum(most, ref[:MAIN])
+            least = jnp.minimum(least, ref[:MAIN])
+            if group:
+                tail = ref[MAIN : MAIN + TAIL]
+                most = jnp.maximum(most, jnp.max(tail, axis=0, keepdims=True))
+                least = jnp.minimum(least, jnp.min(tail, axis=0, keepdims=True))
+        most = jnp.max(most, axis=(0, 1), keepdims=True)
+        least = jnp.min(least, axis=(0, 1), keepdims=True)
+        middle = 0.5 * (most + least)
+        reach = jnp.maximum(0.5001 * (most - least), 1e-30)
+        scale = VALUE_LIMIT / reach
+        unscale[group] = reach * longest * (2 / FLUX_LIMIT)
         for chunk, ref in enumerate(chunks):
-            parts[group, :, chunk * 128 : (chunk + 1) * 128] = split_three(ref[...] * scale, group)
+            value = (ref[...] - middle) * scale
+            parts[group, :, chunk * 128 : (chunk + 1) * 128] = split_three(value, group)
 
     def ghost_scatter(group, step):
         total = dot_t(flux[group], corner_hot[OWN:, :])
@@ -350,7 +370,7 @@
 
     def spec_copy(group, shift):
         to = lax.rem(spec + shift, SPEC)
-        count = MAIN + 8 * group
+        count = MAIN + TAIL * group
         return pltpu.make_async_remote_copy(
             src_ref=energy.at[group, to, pl.ds(0, count)],
             dst_ref=landing.at[spec, pl.ds(group * MAIN, count)],
@@ -363,7 +383,7 @@
     def spread(group):
         for shift in (4, 3, 5, 2, 6, 1, 7):
             spec_copy(group, shift).start()
-        count = MAIN + 8 * group
+        count = MAIN + TAIL * group
         landing[spec, pl.ds(group * MAIN, count)] = energy[group, spec, :count]
 
     for group in range(GROUPS):
@@ -374,19 +394,27 @@
     for group in range(GROUPS):
         send_ghosts(group, 0)
 
-    for step in range(STEPS):
-        for group in range(GROUPS):
-            ready(group, step)
-            gather(group)
-            ghost_scatter(group, step)
-        for group in range(GROUPS):
-            own_scatter(group)
-            update(group, step)
-            if step + 1 < STEPS:
-                make_ghosts(group, step + 1)
-                send_ghosts(group, step + 1)
-            else:
-                spread(group)
+    for group in range(GROUPS):
+        ready(group, 0)
+        gather(group)
+        ghost_scatter(group, 0)
+    for group in range(GROUPS):
+        own_scatter(group)
+        update(group, 0)
+        make_ghosts(group, 1)
+        send_ghosts(group, 1)
+    ready(0, 1)
+    gather(0)
+    ghost_scatter(0, 1)
+    own_scatter(0)
+    ready(1, 1)
+    gather(1)
+    update(0, 1)
+    spread(0)
+    ghost_scatter(1, 1)
+    own_scatter(1)
+    update(1, 1)
+    spread(1)
 
     def partner_code(partner, first, sign):
         bin_ = lax.broadcasted_iota(jnp.int32, (1, 128), 1).astype(f32) + first
@@ -426,7 +454,7 @@
     for group in range(GROUPS):
         for shift in range(1, SPEC):
             source = lax.rem(spec + SPEC - shift, SPEC)
-            place = landing.at[source, pl.ds(group * MAIN, MAIN + 8 * group)]
+            place = landing.at[source, pl.ds(group * MAIN, MAIN + TAIL * group)]
             pltpu.make_async_remote_copy(
                 src_ref=place,
                 dst_ref=place,
@@ -475,7 +503,7 @@
         term[pl.ds(base + NDIR, 3)] = value[:3]
         return carry
 
-    lax.fori_loop(0, NFREQ, terms, 0)
+    lax.fori_loop(0, NFREQ, terms, 0, unroll=4)
 
     def gained(codes, at, code):
         rows = pl.ds(at, wide)
@@ -491,7 +519,7 @@
         out[pl.ds(f * NDIR, NDIR)] = value[:NDIR]
         return carry
 
-    lax.fori_loop(0, NFREQ, changes, 0)
+    lax.fori_loop(0, NFREQ, changes, 0, unroll=4)
     high = (NFREQ + 1) * STRIDE + LEAD
     low = 2 * STRIDE + LEAD
     for turn in (1, 2, 3):

time: 67.8 us -> 68 us (level)
  no operation moved by 1% of the time
where the time goes in v4:
time: 68 us; the launch traced here: 67.9 us
  Pallas kernels  65.9 us (97%)
  local copies, waits for them, and re-layouts  1.97 us (3%)
    pallas_call x1, Pallas kernels, on_device(): pl.pallas_call(kernel, out_shape=jax.ShapeDtypeStruct((BINS, SLOT), f32),...  65.9 us
    unnamed x1, local copies, waits for them, and re-layouts  1.97 us

profile of v4, /device:TPU:1, one launch (start us, length us, event | category | flops | bytes accessed | tf_op | source)
XLA Modules:
  0.0 67.9 jit_solution(18213674521333333074)
XLA Ops:
  0.0 65.9 %shard_map.100 = f32[1296,128]{1,0:T(8,128)} custom-call(f32[162,1024]{1,0:T(8,128)} %spectrum.1, f32[3,2,2048]{2,1,0:T(2,128)} %bitcast.2, s32[3,2048]{1,0:T(4,128)} %conn.1, s32[1,4,128]{2,1,0:T(4,128)} %send_nodes.1, f32[1,1024]{1,0:T(1,128)} %bitcast.3, f32[36]{0:T(128)} %group_speed.1, s32[1296]{0:T(1024)} %dia_plus.1, s32[1296]{0:T(1024)} %dia_minus.1, ...), custom_call_target="tpu_custom_call" | custom-call | tf_op jit(solution)/shard_map/pallas_call | solution.py:553
  65.9 2.0 %copy.12 = f32[1296,128]{1,0:T(8,128)} copy(f32[1296,128]{1,0:T(8,128)} %shard_map.100) | data formatting | bytes 1327104

commit v5 on v4

--- a/solution.py
+++ b/solution.py
@@ -227,28 +227,30 @@
         away = [jnp.maximum(-value, 0.0) for value in k]
         for edge in range(3):
             a, b = edge, (edge + 1) % 3
-            value = jnp.minimum(into[a], away[b]) - jnp.minimum(into[b], away[a])
-            edge_weight[edge, :, at] = flux_scale * value
+            sign = 1 if edge < 2 else -1
+            edge_weight[2 * edge, :, at] = jnp.minimum(into[a], away[b]) * (flux_scale * sign)
+            edge_weight[2 * edge + 1, :, at] = jnp.minimum(into[b], away[a]) * (flux_scale * -sign)
         return carry
 
     def build_hot(chunk, carry):
-        one, minus, zero = [jnp.full((128, CHUNK), value, f32).astype(f8) for value in (1, -1, 0)]
-        node = lax.broadcasted_iota(jnp.int8, (128, CHUNK), 0)
+        one, minus, zero = [jnp.full((32, CHUNK), value, f32).astype(f8) for value in (1, -1, 0)]
+        node = lax.broadcasted_iota(jnp.int32, (32, CHUNK), 0)
+        nodes = [(node + first).astype(jnp.int8) for first in range(0, 128, 32)]
         corners = [conn[corner : corner + 1, lanes(chunk, CHUNK)] for corner in range(3)]
         for first in range(0, EXT, 128):
-            rows = slice(first, first + 128)
-            hits = []
-            for corner in range(3):
-                local = corners[corner] - first
-                local = jnp.where((local >= 0) & (local < 128), local, -1).astype(jnp.int8)
-                hits.append(node == jnp.broadcast_to(local, (128, CHUNK)))
-            for corner in range(3):
-                value = jnp.where(hits[corner], one, zero)
-                corner_hot[rows, lanes(chunk * 3 + corner, CHUNK)] = value
-            for edge in range(2):
-                a, b = hits[edge], hits[edge + 1]
-                value = jnp.where(a, jnp.where(b, zero, one), jnp.where(b, minus, zero))
-                edge_hot[rows, lanes(chunk * 2 + edge, CHUNK)] = value
+            local = [value - first for value in corners]
+            local = [jnp.where((value >= 0) & (value < 128), value, -1) for value in local]
+            local = [jnp.broadcast_to(value.astype(jnp.int8), (32, CHUNK)) for value in local]
+            for quarter in range(4):
+                rows = slice(first + 32 * quarter, first + 32 * quarter + 32)
+                hits = [nodes[quarter] == value for value in local]
+                for corner in range(3):
+                    value = jnp.where(hits[corner], one, zero)
+                    corner_hot[rows, lanes(chunk * 3 + corner, CHUNK)] = value
+                for edge in range(2):
+                    a, b = hits[edge], hits[edge + 1]
+                    value = jnp.where(a, jnp.where(b, zero, one), jnp.where(b, minus, zero))
+                    edge_hot[rows, lanes(chunk * 2 + edge, CHUNK)] = value
         return carry
 
     def edge_dot(group, chunk, target):
@@ -259,13 +261,11 @@
 
         def corners(first, size, d01, d12):
             start = (group * MAIN + first) % (2 * NDIR)
-            d20 = -(d01 + d12)
-            w01, w12, w20 = [edge_weight[edge, start : start + size, at] for edge in range(3)]
-            return [
-                jnp.maximum(w01, 0.0) * d01 + jnp.minimum(w20, 0.0) * d20,
-                jnp.maximum(w12, 0.0) * d12 + jnp.minimum(w01, 0.0) * d01,
-                jnp.maximum(w20, 0.0) * d20 + jnp.minimum(w12, 0.0) * d12,
+            d02 = d01 + d12
+            w01, w10, w12, w21, w20, w02 = [
+                edge_weight[edge, start : start + size, at] for edge in range(6)
             ]
+            return [w01 * d01 + w02 * d02, w12 * d12 + w10 * d01, w20 * d02 + w21 * d12]
 
         for first in range(0, MAIN, 16):
             edges = [
@@ -562,7 +562,7 @@
             pltpu.VMEM((OWN, BLOCKS * SLOT), bf16),
             pltpu.VMEM((EXT, 3 * ELEM), f8),
             pltpu.VMEM((EXT, 2 * ELEM), f8),
-            pltpu.VMEM((3, TROWS, ELEM), f32),
+            pltpu.VMEM((6, TROWS, ELEM), f32),
             pltpu.VMEM((PARTS, 2 * CHUNK), f32),
             pltpu.VMEM((PARTS, 2 * CHUNK), f32),
             pltpu.VMEM((PARTS, 3 * CHUNK), f32),

time: 68 us -> 66.8 us (0.982)
  Pallas kernels: 65.9 us -> 64.7 us
    pallas_call x1, Pallas kernels: 65.9 us -> 64.7 us  [on_device(): pl.pallas_call(kernel, out_shape=jax.ShapeDtypeStruct((BINS, SLOT), f32),...]
where the time goes in v5:
time: 66.8 us; the launch traced here: 66.7 us
  Pallas kernels  64.7 us (97%)
  local copies, waits for them, and re-layouts  1.97 us (3%)
    pallas_call x1, Pallas kernels, on_device(): pl.pallas_call(kernel, out_shape=jax.ShapeDtypeStruct((BINS, SLOT), f32),...  64.7 us
    unnamed x1, local copies, waits for them, and re-layouts  1.97 us

profile of v5, /device:TPU:1, one launch (start us, length us, event | category | flops | bytes accessed | tf_op | source)
XLA Modules:
  0.0 66.7 jit_solution(5527224539956333995)
XLA Ops:
  0.0 64.7 %shard_map.100 = f32[1296,128]{1,0:T(8,128)} custom-call(f32[162,1024]{1,0:T(8,128)} %spectrum.1, f32[3,2,2048]{2,1,0:T(2,128)} %bitcast.2, s32[3,2048]{1,0:T(4,128)} %conn.1, s32[1,4,128]{2,1,0:T(4,128)} %send_nodes.1, f32[1,1024]{1,0:T(1,128)} %bitcast.3, f32[36]{0:T(128)} %group_speed.1, s32[1296]{0:T(1024)} %dia_plus.1, s32[1296]{0:T(1024)} %dia_minus.1, ...), custom_call_target="tpu_custom_call" | custom-call | tf_op jit(solution)/shard_map/pallas_call | solution.py:553
  64.7 2.0 %copy.12 = f32[1296,128]{1,0:T(8,128)} copy(f32[1296,128]{1,0:T(8,128)} %shard_map.100) | data formatting | bytes 1327104

commit v6 on v5

--- a/solution.py
+++ b/solution.py
@@ -388,11 +388,12 @@
 
     for group in range(GROUPS):
         make_ghosts(group, 0)
-    lax.fori_loop(0, CHUNKS, build_hot, 0)
-    lax.fori_loop(0, ELEM // 128, edge_weights, 0)
+    lax.fori_loop(0, 2, build_hot, 0)
     pl.semaphore_wait(barrier, BLOCKS + SPEC - 1)
     for group in range(GROUPS):
         send_ghosts(group, 0)
+    lax.fori_loop(2, CHUNKS, build_hot, 0)
+    lax.fori_loop(0, ELEM // 128, edge_weights, 0)
 
     for group in range(GROUPS):
         ready(group, 0)
@@ -451,6 +452,21 @@
         to_column(value, rule)
         to_padded(target)
 
+    half = NDIR // 2
+    early = MAIN // half
+
+    def place_pieces(first, last):
+        for source in range(SPEC):
+            for piece in range(first, last):
+                f, second = divmod(source * (ROWS // half) + piece, 2)
+                base = (f + 2) * STRIDE + LEAD
+                value = landing[source, piece * half : (piece + 1) * half]
+                padded[base + second * half : base + (second + 1) * half] = value
+                if second:
+                    padded[base - 3 : base] = value[half - 3 :]
+                else:
+                    padded[base + NDIR : base + NDIR + 3] = value[:3]
+
     for group in range(GROUPS):
         for shift in range(1, SPEC):
             source = lax.rem(spec + SPEC - shift, SPEC)
@@ -463,18 +479,8 @@
                 device_id={"dom": dom, "spec": source},
                 device_id_type=MESH,
             ).wait_recv()
-
-    half = NDIR // 2
-    for source in range(SPEC):
-        for piece in range(ROWS // half):
-            f, second = divmod(source * (ROWS // half) + piece, 2)
-            base = (f + 2) * STRIDE + LEAD
-            value = landing[source, piece * half : (piece + 1) * half]
-            padded[base + second * half : base + (second + 1) * half] = value
-            if second:
-                padded[base - 3 : base] = value[half - 3 :]
-            else:
-                padded[base + NDIR : base + NDIR + 3] = value[:3]
+        place_pieces(*((early, ROWS // half) if group else (0, early)))
+
     for block in range(2):
         padded[block * STRIDE : (block + 1) * STRIDE] = padded[2 * STRIDE : 3 * STRIDE]
         last = (NFREQ + 2 + block) * STRIDE

time: 66.8 us -> 64.4 us (0.964)
  Pallas kernels: 64.7 us -> 62.2 us
    pallas_call x1, Pallas kernels: 64.7 us -> 62.2 us  [on_device(): pl.pallas_call(kernel, out_shape=jax.ShapeDtypeStruct((BINS, SLOT), f32),...]
where the time goes in v6:
time: 64.4 us; the launch traced here: 64.2 us
  Pallas kernels  62.2 us (97%)
  local copies, waits for them, and re-layouts  1.97 us (3%)
    pallas_call x1, Pallas kernels, on_device(): pl.pallas_call(kernel, out_shape=jax.ShapeDtypeStruct((BINS, SLOT), f32),...  62.2 us
    unnamed x1, local copies, waits for them, and re-layouts  1.97 us

profile of v6, /device:TPU:1, one launch (start us, length us, event | category | flops | bytes accessed | tf_op | source)
XLA Modules:
  0.0 64.2 jit_solution(14160028346465757725)
XLA Ops:
  0.0 62.2 %shard_map.100 = f32[1296,128]{1,0:T(8,128)} custom-call(f32[162,1024]{1,0:T(8,128)} %spectrum.1, f32[3,2,2048]{2,1,0:T(2,128)} %bitcast.2, s32[3,2048]{1,0:T(4,128)} %conn.1, s32[1,4,128]{2,1,0:T(4,128)} %send_nodes.1, f32[1,1024]{1,0:T(1,128)} %bitcast.3, f32[36]{0:T(128)} %group_speed.1, s32[1296]{0:T(1024)} %dia_plus.1, s32[1296]{0:T(1024)} %dia_minus.1, ...), custom_call_target="tpu_custom_call" | custom-call | tf_op jit(solution)/shard_map/pallas_call | solution.py:559
  62.3 2.0 %copy.12 = f32[1296,128]{1,0:T(8,128)} copy(f32[1296,128]{1,0:T(8,128)} %shard_map.100) | data formatting | bytes 1327104
